TPU v7x, 512 devices: a whole 4x4x16 slice. The times are simulated.
512 devices in a mesh: seq: 128 (over y, z, core), ch: 4 (over x).
Axes of the slice: x: 4, y: 4, z: 16, core: 2. Of those that a mesh axis runs over, the one named last changes fastest.
Arguments:
- signal: bfloat16 [16384, 4096], P('seq', 'ch'), may hold values from -6 to 6
- upstream: bfloat16 [16384, 4096], P('seq', 'ch'), may hold values from -6 to 6
- long_filter: bfloat16 [16384, 4096], P('seq', 'ch'), may hold values from -1 to 1
- short_filter: bfloat16 [128, 256], P(None, 'ch'), may hold values from -0.5 to 0.5
- skip_gain: float32 [4096], P('ch'), may hold values from 0.5 to 1.5
Outputs:
- grad_signal: bfloat16 [16384, 4096], P('seq', 'ch')
- grad_long: bfloat16 [16384, 4096], P('seq', 'ch')
- grad_short: float32 [128, 256], P(None, 'ch')
All inputs are finite; a program needn't handle non-finite values.
Results may differ from a plain program's by a relative error of at most 0.012.
Values may be sent and summed in bfloat16 or wider, within the bound.
No kernel may reach another device: no remote copies, remote signals or barrier semaphores. Data moves between devices by JAX's collectives and lax.ppermute only.
A program may use at most 64 MiB of HBM per device.

v0:
```python
import math

import jax
import jax.numpy as jnp
from jax import lax
from jax.sharding import PartitionSpec as P

GROUP = 16


high_precision = lax.Precision.HIGH
two_pi = 2.0 * math.pi


def shifted(block, axis, distance):
    devices = range(lax.axis_size(axis))
    route = [(i - distance, i) for i in devices if i - distance in devices]
    return lax.ppermute(block, axis, route)


def block_rows(tap_count):
    return min(32, tap_count)


def window_view(extended, block, tap_count):
    groups_here, members, total_rows = extended.shape
    steps_ahead = tap_count // block
    block_count = total_rows // block - steps_ahead
    pieces = extended.reshape(groups_here, members, block_count + steps_ahead, block)
    return jnp.concatenate(
        [pieces[:, :, offset : offset + block_count] for offset in range(steps_ahead + 1)], axis=3
    )


def toeplitz_rows(kernel_taps, block):
    groups_here, tap_count = kernel_taps.shape
    width = block + tap_count
    row_pattern = jnp.concatenate(
        [kernel_taps, jnp.zeros((groups_here, width + 1 - tap_count), kernel_taps.dtype)], axis=1
    )
    tiled = jnp.tile(row_pattern, (1, block))
    return tiled[:, : block * width].reshape(groups_here, block, width)


def window_conv(extended, kernel_taps):
    groups_here, members, total_rows = extended.shape
    tap_count = kernel_taps.shape[1]
    block = block_rows(tap_count)
    windows = window_view(extended, block, tap_count)
    matrix = toeplitz_rows(kernel_taps, block)
    result = jnp.einsum("gcbj,gij->gcbi", windows, matrix, preferred_element_type=jnp.float32)
    return result.reshape(groups_here, members, total_rows - tap_count)


def tap_products(gradients, extended, tap_count):
    groups_here, members, row_count = gradients.shape
    block = block_rows(tap_count)
    width = block + tap_count
    windows = window_view(extended, block, tap_count)
    blocks = gradients.reshape(groups_here, members, row_count // block, block)
    table = jnp.einsum("gcbi,gcbj->gij", blocks, windows, preferred_element_type=jnp.float32)
    flat = table.reshape(groups_here, block * width)
    flat = jnp.concatenate([flat, jnp.zeros((groups_here, block), jnp.float32)], axis=1)
    diagonal = flat.reshape(groups_here, block, width + 1)[:, :, :tap_count]
    return jnp.flip(jnp.sum(diagonal, axis=1), axis=1).T


def phase_table(count_rows, count_cols, modulus):
    grid = (
        lax.broadcasted_iota(jnp.int32, (count_rows, count_cols), 0)
        * lax.broadcasted_iota(jnp.int32, (count_rows, count_cols), 1)
        % modulus
    )
    angle = grid.astype(jnp.float32) * (two_pi / modulus)
    return (jnp.cos(angle), -jnp.sin(angle))


def dft_tables(total):
    first = math.isqrt(total)
    while total % first != 0:
        first = first - 1
    second = total // first
    return (
        first,
        second,
        phase_table(second, second, second),
        phase_table(first, first, first),
        phase_table(second, first, total),
    )


def conjugate(table):
    return (table[0], -table[1])


def complex_mult(left_pair, right_pair):
    left_real, left_imag = left_pair
    right_real, right_imag = right_pair
    return (
        left_real * right_real - left_imag * right_imag,
        left_real * right_imag + left_imag * right_real,
    )


def left_apply(table, real_grid, imag_grid):

    def multiply(matrix, data):
        return jnp.einsum(
            "ku,tux->tkx",
            matrix,
            data,
            precision=high_precision,
            preferred_element_type=jnp.float32,
        )

    if imag_grid is None:
        return (multiply(table[0], real_grid), multiply(table[1], real_grid))
    return (
        multiply(table[0], real_grid) - multiply(table[1], imag_grid),
        multiply(table[0], imag_grid) + multiply(table[1], real_grid),
    )


def right_apply(real_grid, imag_grid, table):

    def multiply(data, matrix):
        return jnp.einsum(
            "snm,mh->snh",
            data,
            matrix,
            precision=high_precision,
            preferred_element_type=jnp.float32,
        )

    return (
        multiply(real_grid, table[0]) - multiply(imag_grid, table[1]),
        multiply(real_grid, table[1]) + multiply(imag_grid, table[0]),
    )


def forward_dft(real_part, imag_part, tables):
    first, second, outer, inner, twist = tables
    count = real_part.shape[0]
    real_grid = real_part.reshape(count, second, first)
    imag_grid = None if imag_part is None else imag_part.reshape(count, second, first)
    section = left_apply(outer, real_grid, imag_grid)
    section = complex_mult(section, twist)
    return right_apply(section[0], section[1], inner)


def inverse_dft(spectrum, tables):
    first, second, outer, inner, twist = tables
    section = right_apply(spectrum[0], spectrum[1], conjugate(inner))
    section = complex_mult(section, conjugate(twist))
    result = left_apply(conjugate(outer), section[0], section[1])
    count = result[0].shape[0]
    total = first * second
    return (result[0].reshape(count, total) / total, result[1].reshape(count, total) / total)


def reverse_frequency(spectrum):
    head = spectrum[:, :1, :]
    head = jnp.concatenate([head[:, :, :1], jnp.flip(head[:, :, 1:], axis=2)], axis=2)
    tail = jnp.flip(spectrum[:, 1:, :], axis=(1, 2))
    return jnp.concatenate([head, tail], axis=1)


def spectral(upstream_here, operand_here, filter_here, skip_here):
    count, seq_length = upstream_here.shape
    tables = dft_tables(2 * seq_length)

    def padded(array):
        return jnp.concatenate(
            [array.astype(jnp.float32), jnp.zeros((count, seq_length), jnp.float32)], axis=1
        )

    packed = forward_dft(padded(filter_here), padded(operand_here), tables)
    cotangent = forward_dft(padded(upstream_here), None, tables)
    mirrored = (reverse_frequency(packed[0]), reverse_frequency(packed[1]))
    back_real, back_imag = inverse_dft(complex_mult(cotangent, mirrored), tables)
    grad_mixed = (
        skip_here[:, None] * upstream_here.astype(jnp.float32) + back_real[:, :seq_length]
    ).astype(jnp.bfloat16)
    raw_long = back_imag[:, :seq_length].astype(jnp.bfloat16)
    return (grad_mixed, raw_long)


def on_device(signal, upstream, long_filter, short_filter, skip_gain):
    seq_rows, channel_count = signal.shape
    part_count = lax.axis_size("seq")
    part_index = lax.axis_index("seq")
    per_device = channel_count // part_count
    tap_count = short_filter.shape[0]
    group_count = short_filter.shape[1]
    seq_length = seq_rows * part_count
    skip_here = lax.dynamic_slice_in_dim(skip_gain, part_index * per_device, per_device)

    def channels_first(rows_array):
        return rows_array.T.reshape(group_count, GROUP, rows_array.shape[0])

    zero_row = jnp.zeros((1, channel_count), jnp.bfloat16)
    edge_rows = shifted(signal[seq_rows - (tap_count - 1) :], "seq", 1)
    extended = channels_first(jnp.concatenate([edge_rows, signal, zero_row], axis=0))
    mixed = window_conv(extended, jnp.flip(short_filter.T, axis=1)).astype(jnp.bfloat16)
    mixed_columns = mixed.reshape(channel_count, seq_rows)
    moved = (
        lax.all_to_all(upstream.T, "seq", split_axis=0, concat_axis=1, tiled=True),
        lax.all_to_all(mixed_columns, "seq", split_axis=0, concat_axis=1, tiled=True),
        lax.all_to_all(long_filter.T, "seq", split_axis=0, concat_axis=1, tiled=True),
    )
    upstream_here, mixed_here, filter_here = [item for item in moved]
    grad_here, raw_here = spectral(upstream_here, mixed_here, filter_here, skip_here)
    moved = (
        lax.all_to_all(grad_here, "seq", split_axis=1, concat_axis=0, tiled=True),
        lax.all_to_all(raw_here, "seq", split_axis=1, concat_axis=0, tiled=True),
    )
    grad_mixed, raw_long = [item.T for item in moved]
    next_rows = shifted(grad_mixed[: tap_count - 1], "seq", -1)
    grad_extended = channels_first(jnp.concatenate([grad_mixed, next_rows, zero_row], axis=0))
    grad_signal = window_conv(grad_extended, short_filter.T).astype(jnp.bfloat16)
    grad_signal = grad_signal.reshape(channel_count, seq_rows).T
    partial_short = tap_products(channels_first(grad_mixed), extended, tap_count)
    summed_short = lax.psum(partial_short, "seq")
    grad_short = summed_short / jnp.sqrt(jnp.float32(GROUP * seq_length))
    raw_wide = raw_long.astype(jnp.float32)
    square_total = lax.psum(jnp.sum(raw_wide * raw_wide), ("seq", "ch"))
    long_rms = jnp.sqrt(square_total / (seq_length * channel_count * lax.axis_size("ch")))
    grad_long = (raw_wide / jnp.maximum(1.0, long_rms)).astype(jnp.bfloat16)
    return (grad_signal, grad_long, grad_short)


def solution(mesh):
    placed = (P("seq", "ch"), P("seq", "ch"), P("seq", "ch"), P(None, "ch"), P("ch"))
    return jax.shard_map(
        on_device,
        mesh=mesh,
        in_specs=placed,
        out_specs=(P("seq", "ch"), P("seq", "ch"), P(None, "ch")),
        check_vma=False,
    )
```

profile of v0, /device:TPU:2, one launch (start us, length us, event | category | flops | bytes accessed | tf_op | source)
XLA Modules:
  0.0 855.8 jit_solution(16360967226881007205)
XLA Ops:
  5.2 21.4 %all-to-all-start = ((bf16[128,8,128]{2,1,0:T(8,128)(2,1)}), bf16[128,8,128]{2,1,0:T(8,128)(2,1)}, u32[]{:S(2)}, u32[]{:S(2)}) async-start(bf16[128,8,128]{2,1,0:T(8,128)(2,1)} %bitcast.1), calls=%async_computation | async-start | bytes 524288 | tf_op jit(solution)/shard_map/all_to_all | solution.py:207
  28.9 2.3 reshape.130
  35.8 3.0 fusion.202
  44.1 5.5 concatenate.46
  49.6 2.7 convolution_convert_fusion.1
  54.1 16.1 %all-to-all-start.1 = ((bf16[128,8,128]{2,1,0:T(8,128)(2,1)}), bf16[128,8,128]{2,1,0:T(8,128)(2,1)S(1)}, u32[]{:S(2)}, u32[]{:S(2)}) async-start(bf16[128,8,128]{2,1,0:T(8,128)(2,1)} %bitcast.161), calls=%async_computation.1 | async-start | bytes 524288 | tf_op jit(solution)/shard_map/all_to_all | solution.py:209
  75.1 18.9 %all-to-all-done.1 = bf16[128,8,128]{2,1,0:T(8,128)(2,1)S(1)} async-done(((bf16[128,8,128]{2,1,0:T(8,128)(2,1)}), bf16[128,8,128]{2,1,0:T(8,128)(2,1)S(1)}, u32[]{:S(2)}, u32[]{:S(2)}) %all-to-all-start.1) | async-done | bytes 262176 | tf_op jit(solution)/shard_map/all_to_all | solution.py:209
  93.9 7.7 all-to-all-start.2
  101.7 2.5 fusion.19
  108.8 15.8 %all-to-all-done.2 = bf16[128,8,128]{2,1,0:T(8,128)(2,1)} async-done(((bf16[128,8,128]{2,1,0:T(8,128)(2,1)}), bf16[128,8,128]{2,1,0:T(8,128)(2,1)}, u32[]{:S(2)}, u32[]{:S(2)}) %all-to-all-start.2) | async-done | bytes 262176 | tf_op jit(solution)/shard_map/all_to_all | solution.py:208
  138.0 9.5 %rev.24 = f32[8,255,128]{2,1,0:T(8,128)} reverse(f32[8,255,128]{2,1,0:T(8,128)} %slice.112), dimensions={1,2} | reverse | bytes 2088960 | tf_op jit(solution)/shard_map/jit(_flip)/rev | solution.py:164
  147.6 9.5 %rev.26 = f32[8,255,128]{2,1,0:T(8,128)} reverse(f32[8,255,128]{2,1,0:T(8,128)} %slice.115), dimensions={1,2} | reverse | bytes 2088960 | tf_op jit(solution)/shard_map/jit(_flip)/rev | solution.py:164
  157.9 3.2 multiply_add_fusion.1
  172.7 6.4 all-to-all-start.3
  183.7 19.2 %all-to-all-done.3 = bf16[8,128,128]{2,0,1:T(8,128)(2,1)S(1)} async-done(((bf16[8,128,128]{2,0,1:T(8,128)(2,1)}), bf16[8,128,128]{2,0,1:T(8,128)(2,1)S(1)}, u32[]{:S(2)}, u32[]{:S(2)}) %all-to-all-start.3) | async-done | bytes 262176 | tf_op jit(solution)/shard_map/all_to_all | solution.py:214
  202.8 7.3 all-to-all-start.4
  211.7 2.3 reshape.133
  217.9 2.6 reshape.123
  220.6 12.8 %all-to-all-done.4 = bf16[8,128,128]{2,0,1:T(8,128)(2,1)} async-done(((bf16[8,128,128]{2,0,1:T(8,128)(2,1)}), bf16[8,128,128]{2,0,1:T(8,128)(2,1)}, u32[]{:S(2)}, u32[]{:S(2)}) %all-to-all-start.4) | async-done | bytes 262176 | tf_op jit(solution)/shard_map/all_to_all | solution.py:215
  235.1 2.9 reshape.124
  238.0 98.4 %psum.14 = f32[]{:T(128)} all-reduce(f32[]{:T(128)} %fusion.14), channel_id=1, replica_groups=mesh['seq'=128,'ch'=4] {'seq','ch'}, use_global_device_ids=true, to_apply=%region_1.2 | all-reduce | flops 1 | bytes 8 | tf_op jit(solution)/shard_map/psum | solution.py:226
  340.5 495.5 %psum.15 = f32[128,64]{0,1:T(8,128)S(1)} all-reduce(f32[128,64]{0,1:T(8,128)S(1)} %bitcast.162), channel_id=1, replica_groups=mesh['seq'=128,'ch'=4] {'seq'}, use_global_device_ids=true, to_apply=%region_3.4 | all-reduce | flops 8192 | bytes 65536 | tf_op jit(solution)/shard_map/psum | solution.py:223
  837.7 3.0 fusion.201
  846.0 5.5 concatenate.54
  (115 shorter events, 79.5 us)
Async XLA Ops:
  1.6 32.8 %collective-permute-start = (bf16[127,1024]{1,0:T(8,128)(2,1)S(1)}, bf16[127,1024]{1,0:T(8,128)(2,1)S(1)}, u32[]{:S(2)}, u32[]{:S(2)}) collective-permute-start(bf16[127,1024]{1,0:T(8,128)(2,1)S(1)} %slice.81), channel_id=1, source_target_pairs={{0,4},{4,8},{8,12},{12,16},{16,20},{20,24},{24,28},{28,32},{32,36}... | collective-permute-start | bytes 780296 | tf_op jit(solution)/shard_map/ppermute | solution.py:18
  5.2 48.9 %all-to-all-start = ((bf16[128,8,128]{2,1,0:T(8,128)(2,1)}), bf16[128,8,128]{2,1,0:T(8,128)(2,1)}, u32[]{:S(2)}, u32[]{:S(2)}) async-start(bf16[128,8,128]{2,1,0:T(8,128)(2,1)} %bitcast.1), calls=%async_computation | async-start | bytes 524288 | tf_op jit(solution)/shard_map/all_to_all | solution.py:207
  27.5 3.7 copy-start.8
  28.9 5.6 copy-start.7
  32.1 2.3 copy-start.10
  49.6 2.7 copy-start
  54.1 39.8 %all-to-all-start.1 = ((bf16[128,8,128]{2,1,0:T(8,128)(2,1)}), bf16[128,8,128]{2,1,0:T(8,128)(2,1)S(1)}, u32[]{:S(2)}, u32[]{:S(2)}) async-start(bf16[128,8,128]{2,1,0:T(8,128)(2,1)} %bitcast.161), calls=%async_computation.1 | async-start | bytes 524288 | tf_op jit(solution)/shard_map/all_to_all | solution.py:209
  93.9 30.6 %all-to-all-start.2 = ((bf16[128,8,128]{2,1,0:T(8,128)(2,1)}), bf16[128,8,128]{2,1,0:T(8,128)(2,1)}, u32[]{:S(2)}, u32[]{:S(2)}) async-start(bf16[128,8,128]{2,1,0:T(8,128)(2,1)} %convert_element_type.146), calls=%async_computation.2 | async-start | bytes 524288 | tf_op jit(solution)/shard_map/all_to_all | solution.py:208
  101.7 3.7 copy-start.4
  124.5 2.5 copy-start.5
  125.6 3.0 copy-start.6
  167.8 3.1 copy-start.12
  172.7 30.1 %all-to-all-start.3 = ((bf16[8,128,128]{2,0,1:T(8,128)(2,1)}), bf16[8,128,128]{2,0,1:T(8,128)(2,1)S(1)}, u32[]{:S(2)}, u32[]{:S(2)}) async-start(bf16[8,128,128]{2,0,1:T(8,128)(2,1)} %fusion.30), calls=%async_computation.3 | async-start | bytes 524288 | tf_op jit(solution)/shard_map/all_to_all | solution.py:214
  182.3 27.8 %copy-start.9 = (bf16[128,64]{0,1:T(8,128)(2,1)S(1)}, bf16[128,64]{0,1:T(8,128)(2,1)}, u32[]{:S(2)}) copy-start(bf16[128,64]{0,1:T(8,128)(2,1)} %param.8) | copy-start | bytes 49156
  202.8 7.3 copy-start.2
  202.8 30.6 %all-to-all-start.4 = ((bf16[8,128,128]{2,0,1:T(8,128)(2,1)}), bf16[8,128,128]{2,0,1:T(8,128)(2,1)}, u32[]{:S(2)}, u32[]{:S(2)}) async-start(bf16[8,128,128]{2,0,1:T(8,128)(2,1)} %slice_bitcast_fusion), calls=%async_computation.4 | async-start | bytes 524288 | tf_op jit(solution)/shard_map/all_to_all | solution.py:215
  211.6 4.4 copy-start.1
  235.1 601.6 %copy-start.11 = (bf16[256]{0:T(256)(128)(2,1)S(1)}, bf16[256]{0:T(256)(128)(2,1)}, u32[]{:S(2)}) copy-start(bf16[256]{0:T(256)(128)(2,1)} %copy-done.10) | copy-start | bytes 1540
  238.0 598.7 %copy-start.3 = (bf16[8,128,128]{2,0,1:T(8,128)(2,1)S(1)}, bf16[8,128,128]{2,0,1:T(8,128)(2,1)}, u32[]{:S(2)}) copy-start(bf16[8,128,128]{2,0,1:T(8,128)(2,1)} %copy-done.2) | copy-start | bytes 786436
  337.1 499.6 %collective-permute-start.1 = (bf16[127,1024]{0,1:T(8,128)(2,1)}, bf16[127,1024]{0,1:T(8,128)(2,1)S(1)}, u32[]{:S(2)}, u32[]{:S(2)}) collective-permute-start(bf16[127,1024]{0,1:T(8,128)(2,1)} %bitcast.154), channel_id=1, source_target_pairs={{4,0},{8,4},{12,8},{16,12},{20,16},{24,20},{28,24},{32,28},{36,32}... | collective-permute-start | bytes 780296 | tf_op jit(solution)/shard_map/ppermute | solution.py:18
where the time goes:
time: 866 us; the launch traced here: 856 us
  blocking collectives  594 us (69%)
  local copies, waits for them, and re-layouts  83.7 us (10%)
  waiting for transfers between devices  66.6 us (8%)
  starting transfers between devices  61.9 us (7%)
  matrix products  39.6 us (5%)
    psum x1, blocking collectives, on_device(): summed_short = lax.psum(partial_short, 'seq')  496 us
    psum x1, blocking collectives, on_device(): square_total = lax.psum(jnp.sum(raw_wide * raw_wide), ('seq', 'ch'))  98.4 us
    all_to_all x1, starting transfers between devices, on_device(): lax.all_to_all(upstream.T, 'seq', split_axis=0, concat_axis=1, tiled=True)  21.4 us
    all_to_all x1, waiting for transfers between devices, on_device(): lax.all_to_all(grad_here, 'seq', split_axis=1, concat_axis=0, tiled=True)  19.2 us
    rev x2, local copies, waits for them, and re-layouts, reverse_frequency(): tail = jnp.flip(spectrum[:, 1:, :], axis=(1, 2))  19.1 us
    all_to_all x1, waiting for transfers between devices, on_device(): lax.all_to_all(long_filter.T, 'seq', split_axis=0, concat_axis=1, tiled=T...  18.9 us
    unnamed x45, local copies, waits for them, and re-layouts  18.3 us
  transfers between devices with their start and end apart: 7, of which 4 were waited for; matrix products, arithmetic and copies ran while one was open for 7% of the time, Pallas kernels for 0%

commit v1 on v0

v1 whole, which is shorter than its diff:
```python
import math

import jax
import jax.numpy as jnp
import numpy as np
from jax import lax
from jax.experimental import pallas as pl
from jax.experimental.pallas import tpu as pltpu
from jax.sharding import PartitionSpec as P

GROUP = 16
F32 = jnp.float32
BF16 = jnp.bfloat16


def split_table(table):
    high = table.astype(BF16)
    low = (table - high.astype(np.float64)).astype(BF16)
    return high, low


def dft_tables(blocks, width):
    total = 2 * blocks * width
    k1 = np.arange(blocks)[:, None] + 0.5
    b = np.arange(blocks)[None, :]
    p = np.arange(width)[None, :]
    angle = 2.0 * np.pi * k1 * b / (2 * blocks)
    enter = np.concatenate([np.cos(angle), -np.sin(angle)], axis=0)
    enter_high, enter_low = split_table(enter)
    enter_both = np.concatenate([enter_high, enter_low], axis=1)
    twist_angle = 2.0 * np.pi * k1 * p / total
    twist = np.stack([np.cos(twist_angle), -np.sin(twist_angle)]).astype(np.float32)
    inner_angle = 2.0 * np.pi * np.arange(width)[:, None] * p / width
    cosine, sine = np.cos(inner_angle), np.sin(inner_angle)
    inner = np.block([[cosine, -sine], [sine, cosine]])
    inner_back = np.block([[cosine, sine], [-sine, cosine]])
    leave = np.concatenate([np.cos(angle).T, -np.sin(angle).T], axis=1) * (2.0 / total)
    leave_both = np.concatenate(split_table(leave), axis=0)
    return enter_both, twist, np.stack(split_table(inner)), np.stack(split_table(inner_back)), leave_both


def split(value):
    high = value.astype(BF16)
    return high, (value - high.astype(F32)).astype(BF16)


def dot(left, right, dims=((1,), (0,))):
    return lax.dot_general(left, right, (dims, ((), ())), preferred_element_type=F32)


def skew(value, step):
    rows, width = value.shape
    row = lax.broadcasted_iota(jnp.int32, value.shape, 0)
    bit = 1
    while bit < rows:
        moved = pltpu.roll(value, (bit * step) % width, 1)
        value = jnp.where((row & bit) != 0, moved, value)
        bit *= 2
    return value


def spectral_kernel(
    got_ref, taps_ref, skip_ref, enter_ref, twist_ref, inner_ref, back_ref, leave_ref,
    out_ref, short_ref, square_ref, rows_ref, made_ref,
):
    blocks, lanes_in, width = got_ref.shape
    count = lanes_in // 3
    rows_ref[...] = got_ref[...].astype(F32).reshape(blocks * lanes_in, width)
    taps = taps_ref[...].astype(F32)
    nothing = jnp.zeros((1, width), F32)
    ahead = jnp.concatenate([nothing, taps], axis=1)
    mix_table = skew(jnp.broadcast_to(ahead, (2 * width, 2 * width)), 1)[:, :width].astype(BF16)
    behind = jnp.concatenate([taps, nothing], axis=1)
    unmix_table = skew(jnp.broadcast_to(behind, (width, 2 * width)), 1).astype(BF16)
    row = lax.broadcasted_iota(jnp.int32, (blocks, width), 0)
    twist_real, twist_imag = twist_ref[0], twist_ref[1]
    table = jnp.zeros((width, 2 * width), F32)
    squares = jnp.zeros((blocks, width), F32)

    for c in range(count):
        signal = rows_ref[pl.ds(c, blocks, stride=lanes_in), :]
        upstream = rows_ref[pl.ds(count + c, blocks, stride=lanes_in), :]
        kernel = rows_ref[pl.ds(2 * count + c, blocks, stride=lanes_in), :]
        before = jnp.where(row == 0, 0.0, pltpu.roll(signal, 1, 0))
        signal_pair = jnp.concatenate([before, signal], axis=1).astype(BF16)
        mixed = dot(signal_pair, mix_table).astype(BF16)
        highs, lows = [], []
        for data in (upstream.astype(BF16), kernel.astype(BF16), mixed):
            grid = dot(enter_ref[...], jnp.concatenate([data, data], axis=0))
            real, imag = grid[:blocks], grid[blocks:]
            turned = jnp.concatenate(
                [real * twist_real - imag * twist_imag, real * twist_imag + imag * twist_real], axis=1
            )
            high, low = split(turned)
            highs.append(high)
            lows.append(low)
        wide = dot(jnp.concatenate(highs + lows, axis=0), inner_ref[0])
        rest = dot(jnp.concatenate(highs, axis=0), inner_ref[1])
        spectra = []
        for i in range(3):
            here = slice(i * blocks, (i + 1) * blocks)
            there = slice((i + 3) * blocks, (i + 4) * blocks)
            total = wide[here] + (wide[there] + rest[here])
            spectra.append((total[:, :width], total[:, width:]))
        up_real, up_imag = spectra[0]
        highs, lows = [], []
        for real, imag in spectra[1:]:
            product = jnp.concatenate([up_real * real + up_imag * imag, up_imag * real - up_real * imag], axis=1)
            high, low = split(product)
            highs.append(high)
            lows.append(low)
        wide = dot(jnp.concatenate(highs + lows, axis=0), back_ref[0])
        rest = dot(jnp.concatenate(highs, axis=0), back_ref[1])
        reals, imags = [], []
        for i in range(2):
            here = slice(i * blocks, (i + 1) * blocks)
            there = slice((i + 2) * blocks, (i + 3) * blocks)
            total = wide[here] + (wide[there] + rest[here])
            real, imag = total[:, :width], total[:, width:]
            reals.append(real * twist_real + imag * twist_imag)
            imags.append(imag * twist_real - real * twist_imag)
        high, low = split(
            jnp.concatenate([jnp.concatenate(reals, axis=1), jnp.concatenate(imags, axis=1)], axis=0)
        )
        wide = dot(leave_ref[...], high)
        result = wide[:blocks] + (wide[blocks:] + dot(leave_ref[:blocks], low))
        raw = result[:, width:].astype(BF16).astype(F32)
        made_ref[pl.ds(c, blocks, stride=2 * count), :] = raw
        squares = squares + raw * raw
        grad = (skip_ref[0, c] * upstream + result[:, :width]).astype(BF16)
        grad_wide = grad.astype(F32)
        after = jnp.where(row == blocks - 1, 0.0, pltpu.roll(grad_wide, blocks - 1, 0))
        grad_pair = jnp.concatenate([grad, after.astype(BF16)], axis=1)
        made_ref[pl.ds(count + c, blocks, stride=2 * count), :] = dot(grad_pair, unmix_table, ((1,), (1,)))
        table = table + dot(grad, signal_pair, ((0,), (0,)))

    out_ref[...] = made_ref[...].reshape(out_ref.shape).astype(BF16)
    lined = skew(pltpu.roll(table, 2 * width - 1, 1), -1)[:, :width]
    short_ref[...] = jnp.broadcast_to(jnp.sum(lined, axis=0, keepdims=True), short_ref.shape)
    square_ref[...] = jnp.broadcast_to(jnp.sum(squares, axis=(0, 1), keepdims=True), square_ref.shape)


def spectral(got, taps, skip):
    blocks, lanes_in, width = got.shape
    count = lanes_in // 3
    vmem = pl.BlockSpec(memory_space=pltpu.VMEM)
    tables = dft_tables(blocks, width)
    return pl.pallas_call(
        spectral_kernel,
        out_shape=(
            jax.ShapeDtypeStruct((blocks, 2 * count, width), BF16),
            jax.ShapeDtypeStruct((8, width), F32),
            jax.ShapeDtypeStruct((8, width), F32),
        ),
        in_specs=[vmem, vmem, pl.BlockSpec(memory_space=pltpu.SMEM)] + [vmem] * 5,
        out_specs=(vmem, vmem, vmem),
        scratch_shapes=[
            pltpu.VMEM((blocks * lanes_in, width), F32),
            pltpu.VMEM((blocks * 2 * count, width), F32),
        ],
        compiler_params=pltpu.CompilerParams(vmem_limit_bytes=40 * 2**20),
        cost_estimate=pl.CostEstimate(flops=6 * 10**9, bytes_accessed=4 * 10**6, transcendentals=0),
    )(got, taps, skip, *[jnp.asarray(t) for t in tables])


def pieces(value):
    first = value.astype(BF16)
    rest = value - first.astype(F32)
    second = rest.astype(BF16)
    third = (rest - second.astype(F32)).astype(BF16)
    return first, second, third


def on_device(signal, upstream, long_filter, short_filter, skip_gain):
    rows, channels = signal.shape
    parts = lax.axis_size("seq")
    here = lax.axis_index("seq")
    slabs = lax.axis_size("ch")
    count = channels // parts
    tap_count, groups = short_filter.shape

    def by_owner(array):
        return array.T.reshape(parts, count, rows)

    sent = jnp.concatenate([by_owner(signal), by_owner(upstream), by_owner(long_filter)], axis=1)
    got = lax.all_to_all(sent, "seq", 0, 0, tiled=True)
    group = here * count // GROUP
    taps = lax.dynamic_slice_in_dim(short_filter.T, group, 1, 0)
    skip = lax.dynamic_slice_in_dim(skip_gain, here * count, count)[None, :]
    made, short_part, square_part = spectral(got, taps, skip)

    first, second, third = pieces(square_part[0])
    lane = lax.broadcasted_iota(jnp.int32, (rows,), 0)
    stat = jnp.where(lane == 0, first, jnp.where(lane == 1, second, third))
    short_first, short_second, _ = pieces(short_part[0])
    extra = jnp.stack([short_first, short_second, stat, stat]).reshape(1, 2, 2, rows)
    back = jnp.concatenate(
        [made.reshape(parts, count, 2, rows), jnp.broadcast_to(extra, (parts, 2, 2, rows))], axis=1
    )
    back = lax.all_to_all(back, "seq", 0, 0, tiled=True)
    stats = back[:, count + 1, 0, :3].astype(F32)
    square_total = jnp.broadcast_to(jnp.sum(stats), (8, 128))
    others = [
        lax.ppermute(square_total, "ch", [(i, (i + step) % slabs) for i in range(slabs)])
        for step in range(1, slabs)
    ]
    raw = back[:, : count // 2].reshape(channels, rows)
    grad_signal = back[:, count // 2 : count].reshape(channels, rows).T
    short = back[:, count, 0].astype(F32) + back[:, count, 1].astype(F32)
    short = jnp.sum(short.reshape(groups, parts // groups, tap_count), axis=1)
    grad_short = jnp.flip(short, axis=1).T / jnp.sqrt(jnp.float32(GROUP * rows * parts))
    for other in others:
        square_total = square_total + other
    long_rms = jnp.sqrt(square_total[0, 0] / (rows * parts * channels * slabs))
    grad_long = (raw.astype(F32) / jnp.maximum(1.0, long_rms)).astype(BF16).T
    return (grad_signal, grad_long, grad_short)


def solution(mesh):
    placed = (P("seq", "ch"), P("seq", "ch"), P("seq", "ch"), P(None, "ch"), P("ch"))
    return jax.shard_map(
        on_device,
        mesh=mesh,
        in_specs=placed,
        out_specs=(P("seq", "ch"), P("seq", "ch"), P(None, "ch")),
        check_vma=False,
    )
```

time: 866 us -> 146 us (0.17)
  the two profiles are of different devices: /device:TPU:2 before, /device:TPU:32 now
where the time goes in v1:
time: 146 us; the launch traced here: 145 us
  blocking collectives  46.3 us (32%)
  waiting for transfers between devices  46.1 us (32%)
  starting transfers between devices  29.5 us (20%)
  Pallas kernels  11.2 us (8%)
  local copies, waits for them, and re-layouts  6.45 us (4%)
  other arithmetic  4.26 us (3%)
  between operations  1.56 us (1%)
    all_to_all x1, blocking collectives, on_device(): back = lax.all_to_all(back, 'seq', 0, 0, tiled=True)  46.3 us
    all_to_all x1, waiting for transfers between devices, on_device(): got = lax.all_to_all(sent, 'seq', 0, 0, tiled=True)  44.1 us
    all_to_all x1, starting transfers between devices, on_device(): got = lax.all_to_all(sent, 'seq', 0, 0, tiled=True)  19.3 us
    pallas_call x1, Pallas kernels, spectral(): pl.pallas_call(spectral_kernel, out_shape=(jax.ShapeDtypeStruct((blocks,...  11.2 us
    ppermute x3, starting transfers between devices, on_device(): lax.ppermute(square_total, 'ch', [(i, (i + step) % slabs) for i in range(...  10.2 us
  transfers between devices with their start and end apart: 4, of which 2 were waited for; matrix products, arithmetic and copies ran while one was open for 2% of the time, Pallas kernels for 0%

profile of v1, /device:TPU:32, one launch (start us, length us, event | category | flops | bytes accessed | tf_op | source)
XLA Modules:
  0.0 145.3 jit_solution(7018563412919088913)
XLA Ops:
  0.7 1.2 copy.20
  1.8 1.1 copy.19
  3.0 0.2 copy.18
  3.1 1.0 pad_maximum_fusion
  4.2 19.3 %all-to-all-start = ((bf16[128,24,128]{2,1,0:T(8,128)(2,1)}), bf16[128,24,128]{2,1,0:T(8,128)(2,1)S(1)}, u32[]{:S(2)}, u32[]{:S(2)}) async-start(bf16[128,24,128]{2,1,0:T(8,128)(2,1)} %pad_maximum_fusion), calls=%async_computation | async-start | bytes 1572864 | tf_op jit(solution)/shard_map/all_to_all | solution.py:186
  23.6 0.8 dynamic-slice_bitcast_fusion.skip_ref
  24.3 44.1 %all-to-all-done.got_ref = bf16[128,24,128]{2,1,0:T(8,128)(2,1)S(1)} async-done(((bf16[128,24,128]{2,1,0:T(8,128)(2,1)}), bf16[128,24,128]{2,1,0:T(8,128)(2,1)S(1)}, u32[]{:S(2)}, u32[]{:S(2)}) %all-to-all-start) | async-done | bytes 786464 | tf_op jit(solution)/shard_map/all_to_all | solution.py:186
  68.4 11.2 %shard_map.121 = (bf16[128,16,128]{2,1,0:T(8,128)(2,1)S(1)}, f32[8,128]{1,0:T(8,128)S(1)}, f32[8,128]{1,0:T(8,128)S(1)}) custom-call(bf16[128,24,128]{2,1,0:T(8,128)(2,1)S(1)} %all-to-all-done.got_ref, bf16[1,128]{1,0:T(2,128)(2,1)S(1)} %dynamic-slice_bitcast_fusion.1.taps_ref, f32[1,8]{1,0:T(1,128)S(1)} %dynamic-slice_bitcast_fusion.skip_ref, ...), custom_call_target="tpu_custom_call" | custom-call | flops 6000000000 | bytes 4000000 | tf_op jit(solution)/shard_map/pallas_call | solution.py:148
  79.7 0.8 pad_maximum_fusion.1
  80.6 46.3 %all_to_all.10 = bf16[128,10,2,128]{3,2,1,0:T(2,128)(2,1)S(1)} all-to-all(bf16[128,10,2,128]{3,2,1,0:T(2,128)(2,1)S(1)} %pad_maximum_fusion.1), channel_id=1, replica_groups=mesh['seq'=128,'ch'=4] {'seq'}, dimensions={0} | all-to-all | bytes 1310720 | tf_op jit(solution)/shard_map/all_to_all | solution.py:200
  126.9 0.7 fusion.2
  127.6 0.6 broadcast_in_dim.16
  128.3 4.7 %collective-permute-start.2 = (f32[8,128]{1,0:T(8,128)S(1)}, f32[8,128]{1,0:T(8,128)S(1)}, u32[]{:S(2)}, u32[]{:S(2)}) collective-permute-start(f32[8,128]{1,0:T(8,128)S(1)} %broadcast_in_dim.16), channel_id=1, source_target_pairs={{0,3},{1,0},{2,1},{3,2},{4,7},{5,4},{6,5},{7,6},{8,11},{9,8},{10,9... | collective-permute-start | bytes 12296 | tf_op jit(solution)/shard_map/ppermute | solution.py:204
  132.9 2.7 %collective-permute-start.1 = (f32[8,128]{1,0:T(8,128)S(1)}, f32[8,128]{1,0:T(8,128)S(1)}, u32[]{:S(2)}, u32[]{:S(2)}) collective-permute-start(f32[8,128]{1,0:T(8,128)S(1)} %broadcast_in_dim.16), channel_id=1, source_target_pairs={{0,2},{1,3},{2,0},{3,1},{4,6},{5,7},{6,4},{7,5},{8,10},{9,11},{10,... | collective-permute-start | bytes 12296 | tf_op jit(solution)/shard_map/ppermute | solution.py:204
  135.7 2.8 %collective-permute-start = (f32[8,128]{1,0:T(8,128)S(1)}, f32[8,128]{1,0:T(8,128)S(1)}, u32[]{:S(2)}, u32[]{:S(2)}) collective-permute-start(f32[8,128]{1,0:T(8,128)S(1)} %broadcast_in_dim.16), channel_id=1, source_target_pairs={{0,1},{1,2},{2,3},{3,0},{4,5},{5,6},{6,7},{7,4},{8,9},{9,10},{10,1... | collective-permute-start | bytes 12296 | tf_op jit(solution)/shard_map/ppermute | solution.py:204
  138.5 0.1 reduce_sum.19
  138.7 0.6 multiply_bitcast_fusion
  139.3 0.2 slice.32
  139.5 0.8 copy.21
  140.4 2.0 %collective-permute-done = f32[8,128]{1,0:T(8,128)S(1)} collective-permute-done((f32[8,128]{1,0:T(8,128)S(1)}, f32[8,128]{1,0:T(8,128)S(1)}, u32[]{:S(2)}, u32[]{:S(2)}) %collective-permute-start) | collective-permute-done | bytes 4128 | tf_op jit(solution)/shard_map/ppermute | solution.py:204
  142.4 0.6 add_add_fusion
  143.0 0.5 slice.29
  144.2 0.2 fusion
  144.4 0.8 copy.22
  (24 shorter events, 0.3 us)
Async XLA Ops:
  0.6 22.9 %copy-start = (bf16[128,64]{0,1:T(8,128)(2,1)S(1)}, bf16[128,64]{0,1:T(8,128)(2,1)}, u32[]{:S(2)}) copy-start(bf16[128,64]{0,1:T(8,128)(2,1)} %param.13) | copy-start | bytes 49156
  0.6 2.3 %copy-start.6 = (bf16[128,1024]{1,0:T(8,128)(2,1)S(1)}, bf16[128,1024]{1,0:T(8,128)(2,1)}, u32[]{:S(2)}) copy-start(bf16[128,1024]{1,0:T(8,128)(2,1)} %param.10) | copy-start | bytes 786436
  4.2 64.2 %copy-start.1 = (bf16[2,256,256]{2,1,0:T(8,128)(2,1)S(1)}, bf16[2,256,256]{2,1,0:T(8,128)(2,1)}, u32[]{:S(2)}) copy-start(bf16[2,256,256]{2,1,0:T(8,128)(2,1)} %constant.55.clone.inner_ref) | copy-start | bytes 786436
  4.2 64.2 %copy-start.2 = (bf16[2,256,256]{2,1,0:T(8,128)(2,1)S(1)}, bf16[2,256,256]{2,1,0:T(8,128)(2,1)}, u32[]{:S(2)}) copy-start(bf16[2,256,256]{2,1,0:T(8,128)(2,1)} %constant.56.clone.back_ref) | copy-start | bytes 786436
  4.2 64.2 %copy-start.3 = (bf16[256,256]{1,0:T(8,128)(2,1)S(1)}, bf16[256,256]{1,0:T(8,128)(2,1)}, u32[]{:S(2)}) copy-start(bf16[256,256]{1,0:T(8,128)(2,1)} %constant.53.clone.enter_ref) | copy-start | bytes 393220
  4.2 64.2 %copy-start.4 = (f32[2,128,128]{2,1,0:T(8,128)S(1)}, f32[2,128,128]{2,1,0:T(8,128)}, u32[]{:S(2)}) copy-start(f32[2,128,128]{2,1,0:T(8,128)} %constant.54.clone.twist_ref) | copy-start | bytes 393220
  4.2 64.2 %copy-start.5 = (bf16[256,256]{1,0:T(8,128)(2,1)S(1)}, bf16[256,256]{1,0:T(8,128)(2,1)}, u32[]{:S(2)}) copy-start(bf16[256,256]{1,0:T(8,128)(2,1)} %constant.57.clone.leave_ref) | copy-start | bytes 393220
  4.2 64.2 %all-to-all-start = ((bf16[128,24,128]{2,1,0:T(8,128)(2,1)}), bf16[128,24,128]{2,1,0:T(8,128)(2,1)S(1)}, u32[]{:S(2)}, u32[]{:S(2)}) async-start(bf16[128,24,128]{2,1,0:T(8,128)(2,1)} %pad_maximum_fusion), calls=%async_computation | async-start | bytes 1572864 | tf_op jit(solution)/shard_map/all_to_all | solution.py:186
  128.3 12.1 %collective-permute-start.2 = (f32[8,128]{1,0:T(8,128)S(1)}, f32[8,128]{1,0:T(8,128)S(1)}, u32[]{:S(2)}, u32[]{:S(2)}) collective-permute-start(f32[8,128]{1,0:T(8,128)S(1)} %broadcast_in_dim.16), channel_id=1, source_target_pairs={{0,3},{1,0},{2,1},{3,2},{4,7},{5,4},{6,5},{7,6},{8,11},{9,8},{10,9... | collective-permute-start | bytes 12296 | tf_op jit(solution)/shard_map/ppermute | solution.py:204
  132.9 7.4 %collective-permute-start.1 = (f32[8,128]{1,0:T(8,128)S(1)}, f32[8,128]{1,0:T(8,128)S(1)}, u32[]{:S(2)}, u32[]{:S(2)}) collective-permute-start(f32[8,128]{1,0:T(8,128)S(1)} %broadcast_in_dim.16), channel_id=1, source_target_pairs={{0,2},{1,3},{2,0},{3,1},{4,6},{5,7},{6,4},{7,5},{8,10},{9,11},{10,... | collective-permute-start | bytes 12296 | tf_op jit(solution)/shard_map/ppermute | solution.py:204
  135.7 6.7 %collective-permute-start = (f32[8,128]{1,0:T(8,128)S(1)}, f32[8,128]{1,0:T(8,128)S(1)}, u32[]{:S(2)}, u32[]{:S(2)}) collective-permute-start(f32[8,128]{1,0:T(8,128)S(1)} %broadcast_in_dim.16), channel_id=1, source_target_pairs={{0,1},{1,2},{2,3},{3,0},{4,5},{5,6},{6,7},{7,4},{8,9},{9,10},{10,1... | collective-permute-start | bytes 12296 | tf_op jit(solution)/shard_map/ppermute | solution.py:204

commit v2 on v1

--- a/solution.py
+++ b/solution.py
@@ -61,10 +61,11 @@
 
 def spectral_kernel(
     got_ref, taps_ref, skip_ref, enter_ref, twist_ref, inner_ref, back_ref, leave_ref,
-    out_ref, short_ref, square_ref, rows_ref, made_ref,
+    out_ref, rows_ref, made_ref,
 ):
     blocks, lanes_in, width = got_ref.shape
     count = lanes_in // 3
+    lanes_out = 2 * count + 2
     rows_ref[...] = got_ref[...].astype(F32).reshape(blocks * lanes_in, width)
     taps = taps_ref[...].astype(F32)
     nothing = jnp.zeros((1, width), F32)
@@ -125,19 +126,29 @@
         wide = dot(leave_ref[...], high)
         result = wide[:blocks] + (wide[blocks:] + dot(leave_ref[:blocks], low))
         raw = result[:, width:].astype(BF16).astype(F32)
-        made_ref[pl.ds(c, blocks, stride=2 * count), :] = raw
+        made_ref[pl.ds(c, blocks, stride=lanes_out), :] = raw
         squares = squares + raw * raw
         grad = (skip_ref[0, c] * upstream + result[:, :width]).astype(BF16)
         grad_wide = grad.astype(F32)
         after = jnp.where(row == blocks - 1, 0.0, pltpu.roll(grad_wide, blocks - 1, 0))
         grad_pair = jnp.concatenate([grad, after.astype(BF16)], axis=1)
-        made_ref[pl.ds(count + c, blocks, stride=2 * count), :] = dot(grad_pair, unmix_table, ((1,), (1,)))
+        made_ref[pl.ds(count + c, blocks, stride=lanes_out), :] = dot(grad_pair, unmix_table, ((1,), (1,)))
         table = table + dot(grad, signal_pair, ((0,), (0,)))
 
+    turned = table.T
+    source = lax.broadcasted_iota(jnp.int32, turned.shape, 0)
+    place = lax.broadcasted_iota(jnp.int32, turned.shape, 1)
+    inside = jnp.logical_and(place < source, source <= place + width)
+    lined = skew(jnp.where(inside, turned, 0.0), -1)
+    short = jnp.sum(lined, axis=0, keepdims=True)
+    short_high = short.astype(BF16).astype(F32)
+    square = jnp.broadcast_to(jnp.sum(squares, axis=(0, 1), keepdims=True), (1, width))
+    square_high = square.astype(BF16).astype(F32)
+    lane = lax.broadcasted_iota(jnp.int32, (1, width), 1)
+    second = jnp.where(lane == 0, square_high, jnp.where(lane == 1, square - square_high, short - short_high))
+    made_ref[pl.ds(2 * count, blocks, stride=lanes_out), :] = jnp.broadcast_to(short_high, (blocks, width))
+    made_ref[pl.ds(2 * count + 1, blocks, stride=lanes_out), :] = jnp.broadcast_to(second, (blocks, width))
     out_ref[...] = made_ref[...].reshape(out_ref.shape).astype(BF16)
-    lined = skew(pltpu.roll(table, 2 * width - 1, 1), -1)[:, :width]
-    short_ref[...] = jnp.broadcast_to(jnp.sum(lined, axis=0, keepdims=True), short_ref.shape)
-    square_ref[...] = jnp.broadcast_to(jnp.sum(squares, axis=(0, 1), keepdims=True), square_ref.shape)
 
 
 def spectral(got, taps, skip):
@@ -147,28 +158,113 @@
     tables = dft_tables(blocks, width)
     return pl.pallas_call(
         spectral_kernel,
-        out_shape=(
-            jax.ShapeDtypeStruct((blocks, 2 * count, width), BF16),
-            jax.ShapeDtypeStruct((8, width), F32),
-            jax.ShapeDtypeStruct((8, width), F32),
-        ),
+        out_shape=jax.ShapeDtypeStruct((blocks, count + 1, 2, width), BF16),
         in_specs=[vmem, vmem, pl.BlockSpec(memory_space=pltpu.SMEM)] + [vmem] * 5,
-        out_specs=(vmem, vmem, vmem),
+        out_specs=vmem,
         scratch_shapes=[
             pltpu.VMEM((blocks * lanes_in, width), F32),
-            pltpu.VMEM((blocks * 2 * count, width), F32),
+            pltpu.VMEM((blocks * (2 * count + 2), width), F32),
         ],
         compiler_params=pltpu.CompilerParams(vmem_limit_bytes=40 * 2**20),
         cost_estimate=pl.CostEstimate(flops=6 * 10**9, bytes_accessed=4 * 10**6, transcendentals=0),
     )(got, taps, skip, *[jnp.asarray(t) for t in tables])
 
 
-def pieces(value):
-    first = value.astype(BF16)
-    rest = value - first.astype(F32)
-    second = rest.astype(BF16)
-    third = (rest - second.astype(F32)).astype(BF16)
-    return first, second, third
+def pack_kernel(first_ref, second_ref, third_ref, out_ref, held_ref, sems):
+    owners, lanes_out, rows = out_ref.shape
+    count = lanes_out // 3
+    copies = [
+        pltpu.make_async_copy(ref, held_ref.at[i], sems.at[i])
+        for i, ref in enumerate((first_ref, second_ref, third_ref))
+    ]
+    for copy in copies:
+        copy.start()
+    for i, copy in enumerate(copies):
+        copy.wait()
+        out_ref[:, i * count : (i + 1) * count, :] = held_ref[i].T.reshape(owners, count, rows)
+
+
+def pack(first, second, third, owners):
+    rows, channels = first.shape
+    hbm = pl.BlockSpec(memory_space=pl.ANY)
+    return pl.pallas_call(
+        pack_kernel,
+        out_shape=jax.ShapeDtypeStruct((owners, 3 * channels // owners, rows), BF16),
+        in_specs=[hbm] * 3,
+        out_specs=pl.BlockSpec(memory_space=pltpu.VMEM),
+        scratch_shapes=[pltpu.VMEM((3, rows, channels), BF16), pltpu.SemaphoreType.DMA((3,))],
+        compiler_params=pltpu.CompilerParams(vmem_limit_bytes=60 * 2**20),
+        cost_estimate=pl.CostEstimate(flops=10**6, bytes_accessed=6 * rows * channels * 2, transcendentals=0),
+    )(first, second, third)
+
+
+def square_kernel(back_ref, out_ref):
+    last = back_ref.shape[1] - 1
+    extra = back_ref[:, last].astype(F32)[:, 1]
+    lane = lax.broadcasted_iota(jnp.int32, extra.shape, 1)
+    total = jnp.sum(jnp.where(lane < 2, extra, 0.0), axis=(0, 1), keepdims=True)
+    out_ref[...] = jnp.broadcast_to(total[None], out_ref.shape)
+
+
+def square_sum(back, slabs):
+    vmem = pl.BlockSpec(memory_space=pltpu.VMEM)
+    return pl.pallas_call(
+        square_kernel,
+        out_shape=jax.ShapeDtypeStruct((slabs, 8, 128), F32),
+        in_specs=[vmem],
+        out_specs=vmem,
+        compiler_params=pltpu.CompilerParams(vmem_limit_bytes=16 * 2**20),
+    )(back)
+
+
+def signal_kernel(scale, back_ref, signal_ref, short_ref):
+    parts, pairs, _, rows = back_ref.shape
+    half = (pairs - 1) // 2
+    channels = signal_ref.shape[1]
+    groups = short_ref.shape[0]
+    signal_ref[...] = back_ref[:, half : 2 * half].astype(F32).reshape(channels, rows).T.astype(BF16)
+    extra = back_ref[:, pairs - 1].astype(F32)
+    high, low = extra[:, 0], extra[:, 1]
+    lane = lax.broadcasted_iota(jnp.int32, low.shape, 1)
+    short = high + jnp.where(lane < 2, 0.0, low)
+    short_ref[...] = jnp.sum(short.reshape(groups, parts // groups, rows), axis=1) * scale
+
+
+def signal_part(back, channels, groups, scale):
+    parts, pairs, _, rows = back.shape
+    vmem = pl.BlockSpec(memory_space=pltpu.VMEM)
+    return pl.pallas_call(
+        lambda *refs: signal_kernel(scale, *refs),
+        out_shape=(
+            jax.ShapeDtypeStruct((rows, channels), BF16),
+            jax.ShapeDtypeStruct((groups, rows), F32),
+        ),
+        in_specs=[vmem],
+        out_specs=(vmem, vmem),
+        compiler_params=pltpu.CompilerParams(vmem_limit_bytes=16 * 2**20),
+        cost_estimate=pl.CostEstimate(flops=10**6, bytes_accessed=4 * rows * channels, transcendentals=0),
+    )(back)
+
+
+def filter_kernel(entries, back_ref, squares_ref, out_ref):
+    half = (back_ref.shape[1] - 1) // 2
+    rows, channels = out_ref.shape
+    mean = jnp.sum(squares_ref[...], axis=0)[:1, :1] * (1.0 / entries)
+    divisor = jnp.maximum(1.0, jnp.sqrt(mean))
+    raw = back_ref[:, :half].astype(F32).reshape(channels, rows)
+    out_ref[...] = (raw / divisor).T.astype(BF16)
+
+
+def filter_part(back, squares, channels, entries):
+    rows = back.shape[3]
+    vmem = pl.BlockSpec(memory_space=pltpu.VMEM)
+    return pl.pallas_call(
+        lambda *refs: filter_kernel(entries, *refs),
+        out_shape=jax.ShapeDtypeStruct((rows, channels), BF16),
+        in_specs=[vmem, vmem],
+        out_specs=vmem,
+        compiler_params=pltpu.CompilerParams(vmem_limit_bytes=16 * 2**20),
+    )(back, squares)
 
 
 def on_device(signal, upstream, long_filter, short_filter, skip_gain):
@@ -177,43 +273,18 @@
     here = lax.axis_index("seq")
     slabs = lax.axis_size("ch")
     count = channels // parts
-    tap_count, groups = short_filter.shape
-
-    def by_owner(array):
-        return array.T.reshape(parts, count, rows)
-
-    sent = jnp.concatenate([by_owner(signal), by_owner(upstream), by_owner(long_filter)], axis=1)
-    got = lax.all_to_all(sent, "seq", 0, 0, tiled=True)
+    groups = short_filter.shape[1]
+
+    got = lax.all_to_all(pack(signal, upstream, long_filter, parts), "seq", 0, 0, tiled=True)
     group = here * count // GROUP
     taps = lax.dynamic_slice_in_dim(short_filter.T, group, 1, 0)
     skip = lax.dynamic_slice_in_dim(skip_gain, here * count, count)[None, :]
-    made, short_part, square_part = spectral(got, taps, skip)
-
-    first, second, third = pieces(square_part[0])
-    lane = lax.broadcasted_iota(jnp.int32, (rows,), 0)
-    stat = jnp.where(lane == 0, first, jnp.where(lane == 1, second, third))
-    short_first, short_second, _ = pieces(short_part[0])
-    extra = jnp.stack([short_first, short_second, stat, stat]).reshape(1, 2, 2, rows)
-    back = jnp.concatenate(
-        [made.reshape(parts, count, 2, rows), jnp.broadcast_to(extra, (parts, 2, 2, rows))], axis=1
-    )
-    back = lax.all_to_all(back, "seq", 0, 0, tiled=True)
-    stats = back[:, count + 1, 0, :3].astype(F32)
-    square_total = jnp.broadcast_to(jnp.sum(stats), (8, 128))
-    others = [
-        lax.ppermute(square_total, "ch", [(i, (i + step) % slabs) for i in range(slabs)])
-        for step in range(1, slabs)
-    ]
-    raw = back[:, : count // 2].reshape(channels, rows)
-    grad_signal = back[:, count // 2 : count].reshape(channels, rows).T
-    short = back[:, count, 0].astype(F32) + back[:, count, 1].astype(F32)
-    short = jnp.sum(short.reshape(groups, parts // groups, tap_count), axis=1)
-    grad_short = jnp.flip(short, axis=1).T / jnp.sqrt(jnp.float32(GROUP * rows * parts))
-    for other in others:
-        square_total = square_total + other
-    long_rms = jnp.sqrt(square_total[0, 0] / (rows * parts * channels * slabs))
-    grad_long = (raw.astype(F32) / jnp.maximum(1.0, long_rms)).astype(BF16).T
-    return (grad_signal, grad_long, grad_short)
+    back = lax.all_to_all(spectral(got, taps, skip), "seq", 0, 0, tiled=True)
+    squares = lax.all_to_all(square_sum(back, slabs), "ch", 0, 0, tiled=True)
+    scale = 1.0 / math.sqrt(GROUP * rows * parts)
+    grad_signal, short = signal_part(back, channels, groups, scale)
+    grad_long = filter_part(back, squares, channels, float(rows * parts * channels * slabs))
+    return (grad_signal, grad_long, short.T)
 
 
 def solution(mesh):

time: 146 us -> 134 us (0.918)
  starting transfers between devices: 29.5 us -> 23.6 us
  local copies, waits for them, and re-layouts: 6.45 us -> 0.82 us
  Pallas kernels: 11.2 us -> 16.8 us
  other arithmetic: 4.26 us -> 0 us
  blocking collectives: 46.3 us -> 43.7 us
  waiting for transfers between devices: 46.1 us -> 48.4 us
    ppermute x3 -> x0, starting transfers between devices: 10.2 us -> none  [on_device(): lax.ppermute(square_total, 'ch', [(i, (i + step) % slabs) for i in range(...]
    pallas_call x1 -> x5, Pallas kernels: 11.2 us -> 16.8 us  [the longest x1 11.6 us: spectral(): pl.pallas_call(spectral_kernel, out_shape=jax.ShapeDtypeStruct((blocks, c...]
    all_to_all x1 -> x2, waiting for transfers between devices: 44.1 us -> 48.4 us  [the longest x1 44.1 us: on_device(): lax.all_to_all(pack(signal, upstream, long_filter, parts), 'seq', 0, 0, t...]
    all_to_all x1 -> x2, starting transfers between devices: 19.3 us -> 23.6 us  [the longest x1 19.3 us: on_device(): lax.all_to_all(pack(signal, upstream, long_filter, parts), 'seq', 0, 0, t...]
    all_to_all x1, blocking collectives: 46.3 us -> 43.7 us  [on_device(): back = lax.all_to_all(spectral(got, taps, skip), 'seq', 0, 0, tiled=True)]
    transpose x3 -> x0, local copies, waits for them, and re-layouts: 2.45 us -> none  [by_owner(): return array.T.reshape(parts, count, rows)]
    ppermute x3 -> x0, waiting for transfers between devices: 2.01 us -> none  [on_device(): lax.ppermute(square_total, 'ch', [(i, (i + step) % slabs) for i in range(...]
    concatenate x2 -> x0, other arithmetic: 1.87 us -> none  [the longest x1 1.02 us: on_device(): jnp.concatenate([by_owner(signal), by_owner(upstream), by_owner(long_filt...]
  transfers between devices with their start and end apart: 4 -> 2, of which waited for: 2 -> 2; matrix products, arithmetic and copies ran while one was open for 2% -> 1% of each run, Pallas kernels for 0% -> 1%
where the time goes in v2:
time: 134 us
  waiting for transfers between devices  48.4 us (36%)
  blocking collectives  43.7 us (33%)
  starting transfers between devices  23.6 us (18%)
  Pallas kernels  16.8 us (13%)
    all_to_all x1, waiting for transfers between devices, on_device(): lax.all_to_all(pack(signal, upstream, long_filter, parts), 'seq', 0, 0, t...  44.1 us
    all_to_all x1, blocking collectives, on_device(): back = lax.all_to_all(spectral(got, taps, skip), 'seq', 0, 0, tiled=True)  43.7 us
    all_to_all x1, starting transfers between devices, on_device(): lax.all_to_all(pack(signal, upstream, long_filter, parts), 'seq', 0, 0, t...  19.3 us
    pallas_call x1, Pallas kernels, spectral(): pl.pallas_call(spectral_kernel, out_shape=jax.ShapeDtypeStruct((blocks, c...  11.6 us
    all_to_all x1, waiting for transfers between devices, on_device(): squares = lax.all_to_all(square_sum(back, slabs), 'ch', 0, 0, tiled=True)  4.3 us
    all_to_all x1, starting transfers between devices, on_device(): squares = lax.all_to_all(square_sum(back, slabs), 'ch', 0, 0, tiled=True)  4.29 us
  transfers between devices with their start and end apart: 2, of which 2 were waited for; matrix products, arithmetic and copies ran while one was open for 1% of the time, Pallas kernels for 1%

profile of v2, /device:TPU:32, one launch (start us, length us, event | category | flops | bytes accessed | tf_op | source)
XLA Modules:
  0.0 134.0 jit_solution(8500884794560639715)
XLA Ops:
  0.6 0.0 copy-start
  0.6 2.2 %shard_map.121 = bf16[128,24,128]{2,1,0:T(8,128)(2,1)} custom-call(bf16[128,1024]{1,0:T(8,128)(2,1)} %first_ref.1, bf16[128,1024]{1,0:T(8,128)(2,1)} %second_ref.1, bf16[128,1024]{1,0:T(8,128)(2,1)} %third_ref.1), custom_call_target="tpu_custom_call" | custom-call | flops 1000000 | bytes 1572864 | tf_op jit(solution)/shard_map/pallas_call | solution.py:190
  2.9 0.0 copy-start.1
  2.9 0.0 copy-start.2
  2.9 0.0 copy-start.3
  2.9 0.0 copy-start.4
  2.9 0.0 copy-start.5
  2.9 19.3 %all-to-all-start = ((bf16[128,24,128]{2,1,0:T(8,128)(2,1)}), bf16[128,24,128]{2,1,0:T(8,128)(2,1)S(1)}, u32[]{:S(2)}, u32[]{:S(2)}) async-start(bf16[128,24,128]{2,1,0:T(8,128)(2,1)} %shard_map.121), calls=%async_computation | async-start | bytes 1572864 | tf_op jit(solution)/shard_map/all_to_all | solution.py:278
  22.3 0.0 copy-done
  22.3 0.8 dynamic-slice_bitcast_fusion.skip_ref
  23.1 44.1 %all-to-all-done.got_ref = bf16[128,24,128]{2,1,0:T(8,128)(2,1)S(1)} async-done(((bf16[128,24,128]{2,1,0:T(8,128)(2,1)}), bf16[128,24,128]{2,1,0:T(8,128)(2,1)S(1)}, u32[]{:S(2)}, u32[]{:S(2)}) %all-to-all-start) | async-done | bytes 786464 | tf_op jit(solution)/shard_map/all_to_all | solution.py:278
  67.1 0.0 copy-done.1
  67.1 0.0 copy-done.2
  67.1 0.0 copy-done.3
  67.1 0.0 copy-done.4
  67.2 0.0 copy-done.5
  67.2 11.6 %shard_map.122 = bf16[128,9,2,128]{3,2,1,0:T(2,128)(2,1)S(1)} custom-call(bf16[128,24,128]{2,1,0:T(8,128)(2,1)S(1)} %all-to-all-done.got_ref, bf16[1,128]{1,0:T(2,128)(2,1)S(1)} %dynamic-slice_bitcast_fusion.1.taps_ref, f32[1,8]{1,0:T(1,128)S(1)} %dynamic-slice_bitcast_fusion.skip_ref, bf16[256,256]{1,0:T(8,128)(2,1)S(1)} %copy-done.3, ...), custom_call_target="tpu_custom_call" | custom-call | flops 6000000000 | bytes 4000000 | tf_op jit(solution)/shard_map/pallas_call | solution.py:159
  78.8 43.7 %all_to_all.15.refs_0_.back_ref = bf16[128,9,2,128]{3,2,1,0:T(2,128)(2,1)S(1)} all-to-all(bf16[128,9,2,128]{3,2,1,0:T(2,128)(2,1)S(1)} %shard_map.122), channel_id=1, replica_groups=mesh['seq'=128,'ch'=4] {'seq'}, dimensions={0} | all-to-all | bytes 1179648 | tf_op jit(solution)/shard_map/all_to_all | solution.py:282
  122.5 0.8 shard_map.124
  123.3 4.3 %all-to-all-start.2 = ((f32[4,8,128]{2,1,0:T(8,128)}), f32[4,8,128]{2,1,0:T(8,128)S(1)}, u32[]{:S(2)}, u32[]{:S(2)}) async-start(f32[4,8,128]{2,1,0:T(8,128)} %shard_map.124), calls=%async_computation.2 | async-start | bytes 32768 | tf_op jit(solution)/shard_map/all_to_all | solution.py:283
  127.6 1.1 shard_map.123
  128.7 4.3 %all-to-all-done.2.refs_1_ = f32[4,8,128]{2,1,0:T(8,128)S(1)} async-done(((f32[4,8,128]{2,1,0:T(8,128)}), f32[4,8,128]{2,1,0:T(8,128)S(1)}, u32[]{:S(2)}, u32[]{:S(2)}) %all-to-all-start.2) | async-done | bytes 16416 | tf_op jit(solution)/shard_map/all_to_all | solution.py:283
  133.0 1.1 shard_map.125
  (1 shorter events, 0.0 us)
Async XLA Ops:
  0.6 21.7 %copy-start = (bf16[128,64]{0,1:T(8,128)(2,1)S(1)}, bf16[128,64]{0,1:T(8,128)(2,1)}, u32[]{:S(2)}) copy-start(bf16[128,64]{0,1:T(8,128)(2,1)} %param.13) | copy-start | bytes 49156
  2.9 64.3 %copy-start.1 = (bf16[2,256,256]{2,1,0:T(8,128)(2,1)S(1)}, bf16[2,256,256]{2,1,0:T(8,128)(2,1)}, u32[]{:S(2)}) copy-start(bf16[2,256,256]{2,1,0:T(8,128)(2,1)} %constant.41.clone.inner_ref) | copy-start | bytes 786436
  2.9 64.2 %copy-start.2 = (bf16[2,256,256]{2,1,0:T(8,128)(2,1)S(1)}, bf16[2,256,256]{2,1,0:T(8,128)(2,1)}, u32[]{:S(2)}) copy-start(bf16[2,256,256]{2,1,0:T(8,128)(2,1)} %constant.42.clone.back_ref) | copy-start | bytes 786436
  2.9 64.2 %copy-start.3 = (bf16[256,256]{1,0:T(8,128)(2,1)S(1)}, bf16[256,256]{1,0:T(8,128)(2,1)}, u32[]{:S(2)}) copy-start(bf16[256,256]{1,0:T(8,128)(2,1)} %constant.39.clone.enter_ref) | copy-start | bytes 393220
  2.9 64.2 %copy-start.4 = (f32[2,128,128]{2,1,0:T(8,128)S(1)}, f32[2,128,128]{2,1,0:T(8,128)}, u32[]{:S(2)}) copy-start(f32[2,128,128]{2,1,0:T(8,128)} %constant.40.clone.twist_ref) | copy-start | bytes 393220
  2.9 64.2 %copy-start.5 = (bf16[256,256]{1,0:T(8,128)(2,1)S(1)}, bf16[256,256]{1,0:T(8,128)(2,1)}, u32[]{:S(2)}) copy-start(bf16[256,256]{1,0:T(8,128)(2,1)} %constant.43.clone.leave_ref) | copy-start | bytes 393220
  2.9 64.2 %all-to-all-start = ((bf16[128,24,128]{2,1,0:T(8,128)(2,1)}), bf16[128,24,128]{2,1,0:T(8,128)(2,1)S(1)}, u32[]{:S(2)}, u32[]{:S(2)}) async-start(bf16[128,24,128]{2,1,0:T(8,128)(2,1)} %shard_map.121), calls=%async_computation | async-start | bytes 1572864 | tf_op jit(solution)/shard_map/all_to_all | solution.py:278
  123.3 9.7 %all-to-all-start.2 = ((f32[4,8,128]{2,1,0:T(8,128)}), f32[4,8,128]{2,1,0:T(8,128)S(1)}, u32[]{:S(2)}, u32[]{:S(2)}) async-start(f32[4,8,128]{2,1,0:T(8,128)} %shard_map.124), calls=%async_computation.2 | async-start | bytes 32768 | tf_op jit(solution)/shard_map/all_to_all | solution.py:283

commit v3 on v2

v3 whole, which is shorter than its diff:
```python
import math

import jax
import jax.numpy as jnp
import numpy as np
from jax import lax
from jax.experimental import pallas as pl
from jax.experimental.pallas import tpu as pltpu
from jax.sharding import PartitionSpec as P

GROUP = 16
F32 = jnp.float32
BF16 = jnp.bfloat16


def split_table(table):
    high = table.astype(BF16)
    low = (table - high.astype(np.float64)).astype(BF16)
    return high, low


def dft_tables(blocks, width):
    total = 2 * blocks * width
    k1 = np.arange(blocks)[:, None] + 0.5
    b = np.arange(blocks)[None, :]
    p = np.arange(width)[None, :]
    angle = 2.0 * np.pi * k1 * b / (2 * blocks)
    enter = np.concatenate([np.cos(angle), -np.sin(angle)], axis=0)
    enter_high, enter_low = split_table(enter)
    enter_both = np.concatenate([enter_high, enter_low], axis=1)
    twist_angle = 2.0 * np.pi * k1 * p / total
    twist = np.stack([np.cos(twist_angle), -np.sin(twist_angle)]).astype(np.float32)
    inner_angle = 2.0 * np.pi * np.arange(width)[:, None] * p / width
    cosine, sine = np.cos(inner_angle), np.sin(inner_angle)
    inner = np.block([[cosine, -sine], [sine, cosine]])
    return enter_both, twist, np.stack(split_table(inner))


def split(value):
    high = value.astype(BF16)
    return high, (value - high.astype(F32)).astype(BF16)


def dot(left, right, dims=((1,), (0,))):
    return lax.dot_general(left, right, (dims, ((), ())), preferred_element_type=F32)


def skew(value, step):
    rows, width = value.shape
    row = lax.broadcasted_iota(jnp.int32, value.shape, 0)
    bit = 1
    while bit < rows:
        moved = pltpu.roll(value, (bit * step) % width, 1)
        value = jnp.where((row & bit) != 0, moved, value)
        bit *= 2
    return value


def three(highs, lows, tables, dims=((1,), (0,))):
    high = jnp.concatenate(highs, axis=0)
    low = jnp.concatenate(lows, axis=0)
    return dot(high, tables[0], dims) + (dot(low, tables[0], dims) + dot(high, tables[1], dims))


def channel_rows(ref, first, stride, blocks):
    return ref[pl.ds(first, blocks, stride=stride), :]


def enter_grid(columns, enter_ref, twist_ref):
    blocks, width = columns[0].shape
    side = jnp.concatenate(columns, axis=1)
    grid = dot(enter_ref[...], jnp.concatenate([side, side], axis=0))
    twist_real, twist_imag = twist_ref[0], twist_ref[1]
    highs, lows = [], []
    for n in range(len(columns)):
        real = grid[:blocks, n * width : (n + 1) * width]
        imag = grid[blocks:, n * width : (n + 1) * width]
        high, low = split(
            jnp.concatenate(
                [real * twist_real - imag * twist_imag, real * twist_imag + imag * twist_real], axis=1
            )
        )
        highs.append(high)
        lows.append(low)
    return highs, lows


def correlate(lefts, rights, enter_ref, twist_ref, inner_ref):
    blocks = lefts[0].shape[0]
    width = lefts[0].shape[1] // 2
    twist_real, twist_imag = twist_ref[0], twist_ref[1]
    highs, lows = [], []
    for left, right in zip(lefts, rights):
        left_real, left_imag = left[:, :width], left[:, width:]
        real, imag = right[:, :width], right[:, width:]
        high, low = split(
            jnp.concatenate(
                [left_real * real + left_imag * imag, left_imag * real - left_real * imag], axis=1
            )
        )
        highs.append(high)
        lows.append(low)
    backs = three(highs, lows, inner_ref, ((1,), (1,)))
    reals, imags = [], []
    for n in range(len(lefts)):
        real = backs[n * blocks : (n + 1) * blocks, :width]
        imag = backs[n * blocks : (n + 1) * blocks, width:]
        reals.append(real * twist_real + imag * twist_imag)
        imags.append(imag * twist_real - real * twist_imag)
    high, low = split(jnp.concatenate([jnp.concatenate(reals, axis=1), jnp.concatenate(imags, axis=1)], axis=0))
    leave = enter_ref[...].T
    wide = dot(leave, high)
    return (wide[:blocks] + (wide[blocks:] + dot(leave[:blocks], low))) * (1.0 / (blocks * width))


def filter_side_kernel(
    got_ref, taps_ref, enter_ref, twist_ref, inner_ref,
    spectrum_ref, raw_ref, square_ref, rows_ref, made_ref,
):
    blocks, lanes_in, width = got_ref.shape
    count = lanes_in // 3
    rows_ref[...] = got_ref[...].astype(F32).reshape(blocks * lanes_in, width)
    ahead = jnp.concatenate([jnp.zeros((1, width), F32), taps_ref[...].astype(F32)], axis=1)
    mix_table = skew(jnp.broadcast_to(ahead, (2 * width, 2 * width)), 1)[:, :width].astype(BF16)
    row = lax.broadcasted_iota(jnp.int32, (blocks, width), 0)
    pairs, columns = [], []
    for c in range(count):
        signal = channel_rows(rows_ref, c, lanes_in, blocks)
        before = jnp.where(row == 0, 0.0, pltpu.roll(signal, 1, 0))
        pairs.append(jnp.concatenate([before, signal], axis=1).astype(BF16))
        columns.append(channel_rows(rows_ref, count + c, lanes_in, blocks).astype(BF16))
    mixed = dot(jnp.concatenate(pairs, axis=0), mix_table).astype(BF16)
    columns += [mixed[c * blocks : (c + 1) * blocks] for c in range(count)]
    highs, lows = enter_grid(columns, enter_ref, twist_ref)
    spectra = three(highs, lows, inner_ref)
    spectrum_ref[...] = spectra[: count * blocks]
    lefts = [spectra[c * blocks : (c + 1) * blocks] for c in range(count)]
    rights = [spectra[(count + c) * blocks : (count + c + 1) * blocks] for c in range(count)]
    result = correlate(lefts, rights, enter_ref, twist_ref, inner_ref)
    squares = jnp.zeros((blocks, width), F32)
    for c in range(count):
        raw = result[:, c * width : (c + 1) * width].astype(BF16).astype(F32)
        made_ref[pl.ds(c, blocks, stride=count), :] = raw
        squares = squares + raw * raw
    raw_ref[...] = made_ref[...].reshape(raw_ref.shape).astype(BF16)
    total = jnp.sum(squares, axis=(0, 1), keepdims=True)
    square_ref[...] = jnp.broadcast_to(total[None], square_ref.shape)


def signal_side_kernel(
    got_ref, spectrum_ref, raw_ref, taps_ref, skip_ref, enter_ref, twist_ref, inner_ref,
    out_ref, short_ref, rows_ref, made_ref,
):
    blocks, pairs_out, _, width = out_ref.shape
    count = pairs_out - 1
    lanes_in = 3 * count
    rows_ref[...] = got_ref[...].astype(F32).reshape(blocks * lanes_in, width)
    behind = jnp.concatenate([taps_ref[...].astype(F32), jnp.zeros((1, width), F32)], axis=1)
    unmix_table = skew(jnp.broadcast_to(behind, (width, 2 * width)), 1).astype(BF16)
    row = lax.broadcasted_iota(jnp.int32, (blocks, width), 0)
    columns = [channel_rows(rows_ref, 2 * count + c, lanes_in, blocks).astype(BF16) for c in range(count)]
    highs, lows = enter_grid(columns, enter_ref, twist_ref)
    spectra = three(highs, lows, inner_ref)
    lefts = [spectrum_ref[c * blocks : (c + 1) * blocks, :] for c in range(count)]
    rights = [spectra[c * blocks : (c + 1) * blocks] for c in range(count)]
    result = correlate(lefts, rights, enter_ref, twist_ref, inner_ref)
    pairs, grads, signals = [], [], []
    for c in range(count):
        upstream = channel_rows(rows_ref, count + c, lanes_in, blocks)
        grad = (skip_ref[0, c] * upstream + result[:, c * width : (c + 1) * width]).astype(BF16)
        after = jnp.where(row == blocks - 1, 0.0, pltpu.roll(grad.astype(F32), blocks - 1, 0))
        pairs.append(jnp.concatenate([grad, after.astype(BF16)], axis=1))
        grads.append(grad)
        signal = channel_rows(rows_ref, c, lanes_in, blocks)
        before = jnp.where(row == 0, 0.0, pltpu.roll(signal, 1, 0))
        signals.append(jnp.concatenate([before, signal], axis=1).astype(BF16))
    made = dot(jnp.concatenate(pairs, axis=0), unmix_table, ((1,), (1,)))
    for c in range(count):
        made_ref[pl.ds(c, blocks, stride=count), :] = made[c * blocks : (c + 1) * blocks]
    half = count // 2
    out_ref[:, :half] = raw_ref[...]
    out_ref[:, half:count] = made_ref[...].reshape(blocks, half, 2, width).astype(BF16)
    out_ref[:, count:] = jnp.zeros((blocks, 1, 2, width), BF16)
    table = dot(jnp.concatenate(grads, axis=0), jnp.concatenate(signals, axis=0), ((0,), (0,)))
    turned = table.T
    source = lax.broadcasted_iota(jnp.int32, turned.shape, 0)
    place = lax.broadcasted_iota(jnp.int32, turned.shape, 1)
    inside = jnp.logical_and(place < source, source <= place + width)
    lined = skew(jnp.where(inside, turned, 0.0), -1)
    short_ref[...] = jnp.broadcast_to(jnp.sum(lined, axis=0, keepdims=True), short_ref.shape)


def filter_side(got, taps, tables, slabs):
    blocks, lanes_in, width = got.shape
    count = lanes_in // 3
    vmem = pl.BlockSpec(memory_space=pltpu.VMEM)
    return pl.pallas_call(
        filter_side_kernel,
        out_shape=(
            jax.ShapeDtypeStruct((count * blocks, 2 * width), F32),
            jax.ShapeDtypeStruct((blocks, count // 2, 2, width), BF16),
            jax.ShapeDtypeStruct((slabs, 8, width), F32),
        ),
        in_specs=[vmem] * 5,
        out_specs=(vmem,) * 3,
        scratch_shapes=[
            pltpu.VMEM((blocks * lanes_in, width), F32),
            pltpu.VMEM((blocks * count, width), F32),
        ],
        compiler_params=pltpu.CompilerParams(vmem_limit_bytes=40 * 2**20),
        cost_estimate=pl.CostEstimate(flops=3 * 10**9, bytes_accessed=6 * 10**6, transcendentals=0),
    )(got, taps, *tables)


def signal_side(got, spectrum, raw, taps, skip, tables):
    blocks, lanes_in, width = got.shape
    count = lanes_in // 3
    vmem = pl.BlockSpec(memory_space=pltpu.VMEM)
    return pl.pallas_call(
        signal_side_kernel,
        out_shape=(
            jax.ShapeDtypeStruct((blocks, count + 1, 2, width), BF16),
            jax.ShapeDtypeStruct((8, width), F32),
        ),
        in_specs=[vmem] * 4 + [pl.BlockSpec(memory_space=pltpu.SMEM)] + [vmem] * 3,
        out_specs=(vmem, vmem),
        scratch_shapes=[
            pltpu.VMEM((blocks * lanes_in, width), F32),
            pltpu.VMEM((blocks * count, width), F32),
        ],
        compiler_params=pltpu.CompilerParams(vmem_limit_bytes=40 * 2**20),
        cost_estimate=pl.CostEstimate(flops=3 * 10**9, bytes_accessed=6 * 10**6, transcendentals=0),
    )(got, spectrum, raw, taps, skip, *tables)


def stamp_kernel(message_ref, short_ref, squares_ref, out_ref, extra_ref, sem):
    del message_ref
    blocks, _, width = extra_ref.shape
    short = short_ref[:1, :]
    short_high = short.astype(BF16).astype(F32)
    square = jnp.sum(squares_ref[...], axis=0)[:1, :]
    square_high = square.astype(BF16).astype(F32)
    lane = lax.broadcasted_iota(jnp.int32, (1, width), 1)
    rest = jnp.where(lane == 0, square_high, jnp.where(lane == 1, square - square_high, short - short_high))
    both = jnp.concatenate([short_high, rest], axis=0)
    extra_ref[...] = jnp.broadcast_to(both[None], extra_ref.shape).astype(BF16)
    copy = pltpu.make_async_copy(extra_ref, out_ref.at[:, out_ref.shape[1] - 1], sem)
    copy.start()
    copy.wait()


def stamp(message, short, squares):
    blocks, _, _, width = message.shape
    vmem = pl.BlockSpec(memory_space=pltpu.VMEM)
    hbm = pl.BlockSpec(memory_space=pl.ANY)
    return pl.pallas_call(
        stamp_kernel,
        out_shape=jax.ShapeDtypeStruct(message.shape, BF16),
        in_specs=[hbm, vmem, vmem],
        out_specs=hbm,
        input_output_aliases={0: 0},
        scratch_shapes=[pltpu.VMEM((blocks, 2, width), BF16), pltpu.SemaphoreType.DMA],
        compiler_params=pltpu.CompilerParams(vmem_limit_bytes=8 * 2**20),
    )(message, short, squares)


def pack_kernel(first_ref, second_ref, third_ref, out_ref, held_ref, sems):
    owners, lanes_out, rows = out_ref.shape
    count = lanes_out // 3
    copies = [
        pltpu.make_async_copy(ref, held_ref.at[i], sems.at[i])
        for i, ref in enumerate((first_ref, second_ref, third_ref))
    ]
    for copy in copies:
        copy.start()
    for i, copy in enumerate(copies):
        copy.wait()
        out_ref[:, i * count : (i + 1) * count, :] = held_ref[i].T.reshape(owners, count, rows)


def pack(first, second, third, owners):
    rows, channels = first.shape
    hbm = pl.BlockSpec(memory_space=pl.ANY)
    return pl.pallas_call(
        pack_kernel,
        out_shape=jax.ShapeDtypeStruct((owners, 3 * channels // owners, rows), BF16),
        in_specs=[hbm] * 3,
        out_specs=pl.BlockSpec(memory_space=pltpu.VMEM),
        scratch_shapes=[pltpu.VMEM((3, rows, channels), BF16), pltpu.SemaphoreType.DMA((3,))],
        compiler_params=pltpu.CompilerParams(vmem_limit_bytes=60 * 2**20),
        cost_estimate=pl.CostEstimate(flops=10**6, bytes_accessed=6 * rows * channels * 2, transcendentals=0),
    )(first, second, third)


def finish_kernel(entries, scale, back_ref, signal_ref, filter_ref, short_ref):
    parts, pairs, _, rows = back_ref.shape
    half = (pairs - 1) // 2
    channels = signal_ref.shape[1]
    groups = short_ref.shape[0]
    extra = back_ref[:, pairs - 1].astype(F32)
    high, low = extra[:, 0], extra[:, 1]
    lane = lax.broadcasted_iota(jnp.int32, low.shape, 1)
    short = high + jnp.where(lane < 2, 0.0, low)
    short_ref[...] = jnp.sum(short.reshape(groups, parts // groups, rows), axis=1) * scale
    squares = jnp.sum(jnp.where(lane < 2, low, 0.0), axis=(0, 1), keepdims=True)
    divisor = jnp.maximum(1.0, jnp.sqrt(squares * (1.0 / entries)))
    signal_ref[...] = back_ref[:, half : 2 * half].astype(F32).reshape(channels, rows).T.astype(BF16)
    raw = back_ref[:, :half].astype(F32).reshape(channels, rows)
    filter_ref[...] = (raw / divisor).T.astype(BF16)


def finish(back, channels, groups, entries, scale):
    rows = back.shape[3]
    vmem = pl.BlockSpec(memory_space=pltpu.VMEM)
    return pl.pallas_call(
        lambda *refs: finish_kernel(entries, scale, *refs),
        out_shape=(
            jax.ShapeDtypeStruct((rows, channels), BF16),
            jax.ShapeDtypeStruct((rows, channels), BF16),
            jax.ShapeDtypeStruct((groups, rows), F32),
        ),
        in_specs=[vmem],
        out_specs=(vmem, vmem, vmem),
        compiler_params=pltpu.CompilerParams(vmem_limit_bytes=16 * 2**20),
    )(back)


def on_device(signal, upstream, long_filter, short_filter, skip_gain):
    rows, channels = signal.shape
    parts = lax.axis_size("seq")
    here = lax.axis_index("seq")
    slabs = lax.axis_size("ch")
    count = channels // parts
    groups = short_filter.shape[1]
    tables = [jnp.asarray(table) for table in dft_tables(parts, rows)]

    got = lax.all_to_all(pack(signal, upstream, long_filter, parts), "seq", 0, 0, tiled=True)
    group = here * count // GROUP
    taps = lax.dynamic_slice_in_dim(short_filter.T, group, 1, 0)
    skip = lax.dynamic_slice_in_dim(skip_gain, here * count, count)[None, :]
    spectrum, raw, squares = filter_side(got, taps, tables, slabs)
    squares = lax.all_to_all(squares, "ch", 0, 0, tiled=True)
    message, short = signal_side(got, spectrum, raw, taps, skip, tables)
    back = lax.all_to_all(stamp(message, short, squares), "seq", 0, 0, tiled=True)
    entries = float(rows * parts * channels * slabs)
    scale = 1.0 / math.sqrt(GROUP * rows * parts)
    grad_signal, grad_long, short = finish(back, channels, groups, entries, scale)
    return (grad_signal, grad_long, short.T)


def solution(mesh):
    placed = (P("seq", "ch"), P("seq", "ch"), P("seq", "ch"), P(None, "ch"), P("ch"))
    return jax.shard_map(
        on_device,
        mesh=mesh,
        in_specs=placed,
        out_specs=(P("seq", "ch"), P("seq", "ch"), P(None, "ch")),
        check_vma=False,
    )
```

time: 134 us -> 127 us (0.948)
  Pallas kernels: 16.8 us -> 12.4 us
  waiting for transfers between devices: 48.4 us -> 45.6 us
    pallas_call x4, Pallas kernels: 14.5 us -> 10.2 us  [the longest x1 4.76 us: filter_side(): pl.pallas_call(filter_side_kernel, out_shape=(jax.ShapeDtypeStruct((count...]
    all_to_all x1, waiting for transfers between devices: 4.3 us -> 1.48 us  [on_device(): squares = lax.all_to_all(squares, 'ch', 0, 0, tiled=True)]
  transfers between devices with their start and end apart: 2 -> 2, of which waited for: 2 -> 2; matrix products, arithmetic and copies ran while one was open for 1% -> 1% of each run, Pallas kernels for 1% -> 3%
where the time goes in v3:
time: 127 us
  waiting for transfers between devices  45.6 us (36%)
  blocking collectives  43.7 us (34%)
  starting transfers between devices  23.6 us (19%)
  Pallas kernels  12.4 us (10%)
    all_to_all x1, waiting for transfers between devices, on_device(): lax.all_to_all(pack(signal, upstream, long_filter, parts), 'seq', 0, 0, t...  44.1 us
    all_to_all x1, blocking collectives, on_device(): lax.all_to_all(stamp(message, short, squares), 'seq', 0, 0, tiled=True)  43.7 us
    all_to_all x1, starting transfers between devices, on_device(): lax.all_to_all(pack(signal, upstream, long_filter, parts), 'seq', 0, 0, t...  19.3 us
    pallas_call x1, Pallas kernels, filter_side(): pl.pallas_call(filter_side_kernel, out_shape=(jax.ShapeDtypeStruct((count...  4.76 us
    all_to_all x1, starting transfers between devices, on_device(): squares = lax.all_to_all(squares, 'ch', 0, 0, tiled=True)  4.29 us
    pallas_call x1, Pallas kernels, signal_side(): pl.pallas_call(signal_side_kernel, out_shape=(jax.ShapeDtypeStruct((block...  3.88 us
  transfers between devices with their start and end apart: 2, of which 2 were waited for; matrix products, arithmetic and copies ran while one was open for 1% of the time, Pallas kernels for 3%

profile of v3, /device:TPU:32, one launch (start us, length us, event | category | flops | bytes accessed | tf_op | source)
XLA Modules:
  0.0 126.8 jit_solution(7251841592055137895)
XLA Ops:
  0.6 0.0 copy-start
  0.6 2.2 %shard_map.103 = bf16[128,24,128]{2,1,0:T(8,128)(2,1)} custom-call(bf16[128,1024]{1,0:T(8,128)(2,1)} %first_ref.1, bf16[128,1024]{1,0:T(8,128)(2,1)} %second_ref.1, bf16[128,1024]{1,0:T(8,128)(2,1)} %third_ref.1), custom_call_target="tpu_custom_call" | custom-call | flops 1000000 | bytes 1572864 | tf_op jit(solution)/shard_map/pallas_call | solution.py:284
  2.9 0.0 copy-start.1
  2.9 0.0 copy-start.2
  2.9 0.0 copy-start.3
  2.9 19.3 %all-to-all-start = ((bf16[128,24,128]{2,1,0:T(8,128)(2,1)}), bf16[128,24,128]{2,1,0:T(8,128)(2,1)S(1)}, u32[]{:S(2)}, u32[]{:S(2)}) async-start(bf16[128,24,128]{2,1,0:T(8,128)(2,1)} %shard_map.103), calls=%async_computation | async-start | bytes 1572864 | tf_op jit(solution)/shard_map/all_to_all | solution.py:337
  22.3 0.8 dynamic-slice_bitcast_fusion.skip_ref
  23.0 0.0 copy-done
  23.0 44.1 %all-to-all-done.got_ref = bf16[128,24,128]{2,1,0:T(8,128)(2,1)S(1)} async-done(((bf16[128,24,128]{2,1,0:T(8,128)(2,1)}), bf16[128,24,128]{2,1,0:T(8,128)(2,1)S(1)}, u32[]{:S(2)}, u32[]{:S(2)}) %all-to-all-start) | async-done | bytes 786464 | tf_op jit(solution)/shard_map/all_to_all | solution.py:337
  67.1 0.0 copy-done.1
  67.1 0.0 copy-done.2
  67.1 0.0 copy-done.3
  67.1 4.8 %shard_map.104 = (f32[1024,256]{1,0:T(8,128)S(1)}, bf16[128,4,2,128]{3,2,1,0:T(2,128)(2,1)S(1)}, f32[4,8,128]{2,1,0:T(8,128)}) custom-call(bf16[128,24,128]{2,1,0:T(8,128)(2,1)S(1)} %all-to-all-done.got_ref, bf16[1,128]{1,0:T(2,128)(2,1)S(1)} %dynamic-slice_bitcast_fusion.1.taps_ref, bf16[256,256]{1,0:T(8,128)(2,1)S(1)} %copy-done.3, ...), custom_call_target="tpu_custom_call" | custom-call | flops 3000000000 | bytes 6000000 | tf_op jit(solution)/shard_map/pallas_call | solution.py:197
  71.9 4.3 %all-to-all-start.1 = ((f32[4,8,128]{2,1,0:T(8,128)}), f32[4,8,128]{2,1,0:T(8,128)S(1)}, u32[]{:S(2)}, u32[]{:S(2)}) async-start(f32[4,8,128]{2,1,0:T(8,128)} %get-tuple-element.15), calls=%async_computation.1 | async-start | bytes 32768 | tf_op jit(solution)/shard_map/all_to_all | solution.py:342
  76.2 3.9 %shard_map.105 = (bf16[128,9,2,128]{3,2,1,0:T(2,128)(2,1)S(1)}, f32[8,128]{1,0:T(8,128)S(1)}) custom-call(bf16[128,24,128]{2,1,0:T(8,128)(2,1)S(1)} %all-to-all-done.got_ref, f32[1024,256]{1,0:T(8,128)S(1)} %get-tuple-element.11.spectrum_ref, bf16[128,4,2,128]{3,2,1,0:T(2,128)(2,1)S(1)} %get-tuple-element.12.raw_ref, ...), custom_call_target="tpu_custom_call" | custom-call | flops 3000000000 | bytes 6000000 | tf_op jit(solution)/shard_map/pallas_call | solution.py:219
  80.1 1.5 %all-to-all-done.1.squares_ref = f32[4,8,128]{2,1,0:T(8,128)S(1)} async-done(((f32[4,8,128]{2,1,0:T(8,128)}), f32[4,8,128]{2,1,0:T(8,128)S(1)}, u32[]{:S(2)}, u32[]{:S(2)}) %all-to-all-start.1) | async-done | bytes 16416 | tf_op jit(solution)/shard_map/all_to_all | solution.py:342
  81.5 0.1 shard_map.106
  81.6 43.7 %all_to_all.15.refs_0_ = bf16[128,9,2,128]{3,2,1,0:T(2,128)(2,1)S(1)} all-to-all(bf16[128,9,2,128]{3,2,1,0:T(2,128)(2,1)S(1)} %shard_map.106), channel_id=1, replica_groups=mesh['seq'=128,'ch'=4] {'seq'}, dimensions={0} | all-to-all | bytes 1179648 | tf_op jit(solution)/shard_map/all_to_all | solution.py:344
  125.4 1.5 %shard_map.107 = (bf16[128,1024]{1,0:T(8,128)(2,1)}, bf16[128,1024]{1,0:T(8,128)(2,1)}, f32[64,128]{1,0:T(8,128)}) custom-call(bf16[128,9,2,128]{3,2,1,0:T(2,128)(2,1)S(1)} %all_to_all.15.refs_0_), custom_call_target="tpu_custom_call" | custom-call | tf_op jit(solution)/shard_map/pallas_call | solution.py:315
  (1 shorter events, 0.0 us)
Async XLA Ops:
  0.6 22.4 %copy-start = (bf16[128,64]{0,1:T(8,128)(2,1)S(1)}, bf16[128,64]{0,1:T(8,128)(2,1)}, u32[]{:S(2)}) copy-start(bf16[128,64]{0,1:T(8,128)(2,1)} %param.11) | copy-start | bytes 49156
  2.9 64.2 %copy-start.1 = (bf16[2,256,256]{2,1,0:T(8,128)(2,1)S(1)}, bf16[2,256,256]{2,1,0:T(8,128)(2,1)}, u32[]{:S(2)}) copy-start(bf16[2,256,256]{2,1,0:T(8,128)(2,1)} %constant.37.clone.inner_ref) | copy-start | bytes 786436
  2.9 64.2 %copy-start.2 = (f32[2,128,128]{2,1,0:T(8,128)S(1)}, f32[2,128,128]{2,1,0:T(8,128)}, u32[]{:S(2)}) copy-start(f32[2,128,128]{2,1,0:T(8,128)} %constant.36.clone.twist_ref) | copy-start | bytes 393220
  2.9 64.2 %copy-start.3 = (bf16[256,256]{1,0:T(8,128)(2,1)S(1)}, bf16[256,256]{1,0:T(8,128)(2,1)}, u32[]{:S(2)}) copy-start(bf16[256,256]{1,0:T(8,128)(2,1)} %constant.35.clone.enter_ref) | copy-start | bytes 393220
  2.9 64.2 %all-to-all-start = ((bf16[128,24,128]{2,1,0:T(8,128)(2,1)}), bf16[128,24,128]{2,1,0:T(8,128)(2,1)S(1)}, u32[]{:S(2)}, u32[]{:S(2)}) async-start(bf16[128,24,128]{2,1,0:T(8,128)(2,1)} %shard_map.103), calls=%async_computation | async-start | bytes 1572864 | tf_op jit(solution)/shard_map/all_to_all | solution.py:337
  71.9 9.7 %all-to-all-start.1 = ((f32[4,8,128]{2,1,0:T(8,128)}), f32[4,8,128]{2,1,0:T(8,128)S(1)}, u32[]{:S(2)}, u32[]{:S(2)}) async-start(f32[4,8,128]{2,1,0:T(8,128)} %get-tuple-element.15), calls=%async_computation.1 | async-start | bytes 32768 | tf_op jit(solution)/shard_map/all_to_all | solution.py:342

commit v4 on v3

--- a/solution.py
+++ b/solution.py
@@ -54,6 +54,16 @@
         value = jnp.where((row & bit) != 0, moved, value)
         bit *= 2
     return value
+
+
+def group_taps(taps_ref, count):
+    group = lax.axis_index("seq") * count // GROUP
+    row = lax.broadcasted_iota(jnp.int32, taps_ref.shape, 0)
+    return jnp.sum(jnp.where(row == group, taps_ref[...].astype(F32), 0.0), axis=0, keepdims=True)
+
+
+def slide(line, rows):
+    return pltpu.roll(jnp.broadcast_to(line, (rows, line.shape[1])), 0, 1, stride=1, stride_axis=0)
 
 
 def three(highs, lows, tables, dims=((1,), (0,))):
@@ -115,20 +125,21 @@
 
 def filter_side_kernel(
     got_ref, taps_ref, enter_ref, twist_ref, inner_ref,
-    spectrum_ref, raw_ref, square_ref, rows_ref, made_ref,
+    spectrum_ref, raw_ref, square_ref, rows_ref,
 ):
     blocks, lanes_in, width = got_ref.shape
     count = lanes_in // 3
-    rows_ref[...] = got_ref[...].astype(F32).reshape(blocks * lanes_in, width)
-    ahead = jnp.concatenate([jnp.zeros((1, width), F32), taps_ref[...].astype(F32)], axis=1)
-    mix_table = skew(jnp.broadcast_to(ahead, (2 * width, 2 * width)), 1)[:, :width].astype(BF16)
+    lanes_here = 2 * count
+    rows_ref[...] = got_ref[:, :lanes_here].astype(F32).reshape(blocks * lanes_here, width)
+    ahead = jnp.concatenate([jnp.zeros((1, width), F32), group_taps(taps_ref, count)], axis=1)
+    mix_table = slide(ahead, 2 * width)[:, :width].astype(BF16)
     row = lax.broadcasted_iota(jnp.int32, (blocks, width), 0)
     pairs, columns = [], []
     for c in range(count):
-        signal = channel_rows(rows_ref, c, lanes_in, blocks)
+        signal = channel_rows(rows_ref, c, lanes_here, blocks)
         before = jnp.where(row == 0, 0.0, pltpu.roll(signal, 1, 0))
         pairs.append(jnp.concatenate([before, signal], axis=1).astype(BF16))
-        columns.append(channel_rows(rows_ref, count + c, lanes_in, blocks).astype(BF16))
+        columns.append(channel_rows(rows_ref, count + c, lanes_here, blocks).astype(BF16))
     mixed = dot(jnp.concatenate(pairs, axis=0), mix_table).astype(BF16)
     columns += [mixed[c * blocks : (c + 1) * blocks] for c in range(count)]
     highs, lows = enter_grid(columns, enter_ref, twist_ref)
@@ -139,10 +150,9 @@
     result = correlate(lefts, rights, enter_ref, twist_ref, inner_ref)
     squares = jnp.zeros((blocks, width), F32)
     for c in range(count):
-        raw = result[:, c * width : (c + 1) * width].astype(BF16).astype(F32)
-        made_ref[pl.ds(c, blocks, stride=count), :] = raw
-        squares = squares + raw * raw
-    raw_ref[...] = made_ref[...].reshape(raw_ref.shape).astype(BF16)
+        raw = result[:, c * width : (c + 1) * width].astype(BF16)
+        raw_ref[c] = raw
+        squares = squares + raw.astype(F32) * raw.astype(F32)
     total = jnp.sum(squares, axis=(0, 1), keepdims=True)
     square_ref[...] = jnp.broadcast_to(total[None], square_ref.shape)
 
@@ -155,8 +165,8 @@
     count = pairs_out - 1
     lanes_in = 3 * count
     rows_ref[...] = got_ref[...].astype(F32).reshape(blocks * lanes_in, width)
-    behind = jnp.concatenate([taps_ref[...].astype(F32), jnp.zeros((1, width), F32)], axis=1)
-    unmix_table = skew(jnp.broadcast_to(behind, (width, 2 * width)), 1).astype(BF16)
+    behind = jnp.concatenate([group_taps(taps_ref, count), jnp.zeros((1, width), F32)], axis=1)
+    unmix_table = slide(behind, width).astype(BF16)
     row = lax.broadcasted_iota(jnp.int32, (blocks, width), 0)
     columns = [channel_rows(rows_ref, 2 * count + c, lanes_in, blocks).astype(BF16) for c in range(count)]
     highs, lows = enter_grid(columns, enter_ref, twist_ref)
@@ -164,10 +174,11 @@
     lefts = [spectrum_ref[c * blocks : (c + 1) * blocks, :] for c in range(count)]
     rights = [spectra[c * blocks : (c + 1) * blocks] for c in range(count)]
     result = correlate(lefts, rights, enter_ref, twist_ref, inner_ref)
+    first = lax.axis_index("seq") * count
     pairs, grads, signals = [], [], []
     for c in range(count):
         upstream = channel_rows(rows_ref, count + c, lanes_in, blocks)
-        grad = (skip_ref[0, c] * upstream + result[:, c * width : (c + 1) * width]).astype(BF16)
+        grad = (skip_ref[first + c] * upstream + result[:, c * width : (c + 1) * width]).astype(BF16)
         after = jnp.where(row == blocks - 1, 0.0, pltpu.roll(grad.astype(F32), blocks - 1, 0))
         pairs.append(jnp.concatenate([grad, after.astype(BF16)], axis=1))
         grads.append(grad)
@@ -176,10 +187,9 @@
         signals.append(jnp.concatenate([before, signal], axis=1).astype(BF16))
     made = dot(jnp.concatenate(pairs, axis=0), unmix_table, ((1,), (1,)))
     for c in range(count):
-        made_ref[pl.ds(c, blocks, stride=count), :] = made[c * blocks : (c + 1) * blocks]
-    half = count // 2
-    out_ref[:, :half] = raw_ref[...]
-    out_ref[:, half:count] = made_ref[...].reshape(blocks, half, 2, width).astype(BF16)
+        made_ref[pl.ds(c, blocks, stride=2 * count), :] = raw_ref[c].astype(F32)
+        made_ref[pl.ds(count + c, blocks, stride=2 * count), :] = made[c * blocks : (c + 1) * blocks]
+    out_ref[:, :count] = made_ref[...].reshape(blocks, count, 2, width).astype(BF16)
     out_ref[:, count:] = jnp.zeros((blocks, 1, 2, width), BF16)
     table = dot(jnp.concatenate(grads, axis=0), jnp.concatenate(signals, axis=0), ((0,), (0,)))
     turned = table.T
@@ -198,14 +208,13 @@
         filter_side_kernel,
         out_shape=(
             jax.ShapeDtypeStruct((count * blocks, 2 * width), F32),
-            jax.ShapeDtypeStruct((blocks, count // 2, 2, width), BF16),
+            jax.ShapeDtypeStruct((count, blocks, width), BF16),
             jax.ShapeDtypeStruct((slabs, 8, width), F32),
         ),
         in_specs=[vmem] * 5,
         out_specs=(vmem,) * 3,
         scratch_shapes=[
-            pltpu.VMEM((blocks * lanes_in, width), F32),
-            pltpu.VMEM((blocks * count, width), F32),
+            pltpu.VMEM((blocks * 2 * count, width), F32),
         ],
         compiler_params=pltpu.CompilerParams(vmem_limit_bytes=40 * 2**20),
         cost_estimate=pl.CostEstimate(flops=3 * 10**9, bytes_accessed=6 * 10**6, transcendentals=0),
@@ -226,7 +235,7 @@
         out_specs=(vmem, vmem),
         scratch_shapes=[
             pltpu.VMEM((blocks * lanes_in, width), F32),
-            pltpu.VMEM((blocks * count, width), F32),
+            pltpu.VMEM((blocks * 2 * count, width), F32),
         ],
         compiler_params=pltpu.CompilerParams(vmem_limit_bytes=40 * 2**20),
         cost_estimate=pl.CostEstimate(flops=3 * 10**9, bytes_accessed=6 * 10**6, transcendentals=0),
@@ -281,13 +290,14 @@
 def pack(first, second, third, owners):
     rows, channels = first.shape
     hbm = pl.BlockSpec(memory_space=pl.ANY)
+    first, second, third = [pltpu.with_memory_space_constraint(x, pltpu.HBM) for x in (first, second, third)]
     return pl.pallas_call(
         pack_kernel,
         out_shape=jax.ShapeDtypeStruct((owners, 3 * channels // owners, rows), BF16),
         in_specs=[hbm] * 3,
         out_specs=pl.BlockSpec(memory_space=pltpu.VMEM),
         scratch_shapes=[pltpu.VMEM((3, rows, channels), BF16), pltpu.SemaphoreType.DMA((3,))],
-        compiler_params=pltpu.CompilerParams(vmem_limit_bytes=60 * 2**20),
+        compiler_params=pltpu.CompilerParams(vmem_limit_bytes=16 * 2**20),
         cost_estimate=pl.CostEstimate(flops=10**6, bytes_accessed=6 * rows * channels * 2, transcendentals=0),
     )(first, second, third)
 
@@ -328,19 +338,16 @@
 def on_device(signal, upstream, long_filter, short_filter, skip_gain):
     rows, channels = signal.shape
     parts = lax.axis_size("seq")
-    here = lax.axis_index("seq")
     slabs = lax.axis_size("ch")
     count = channels // parts
     groups = short_filter.shape[1]
     tables = [jnp.asarray(table) for table in dft_tables(parts, rows)]
 
     got = lax.all_to_all(pack(signal, upstream, long_filter, parts), "seq", 0, 0, tiled=True)
-    group = here * count // GROUP
-    taps = lax.dynamic_slice_in_dim(short_filter.T, group, 1, 0)
-    skip = lax.dynamic_slice_in_dim(skip_gain, here * count, count)[None, :]
+    taps = short_filter.T
     spectrum, raw, squares = filter_side(got, taps, tables, slabs)
     squares = lax.all_to_all(squares, "ch", 0, 0, tiled=True)
-    message, short = signal_side(got, spectrum, raw, taps, skip, tables)
+    message, short = signal_side(got, spectrum, raw, taps, skip_gain, tables)
     back = lax.all_to_all(stamp(message, short, squares), "seq", 0, 0, tiled=True)
     entries = float(rows * parts * channels * slabs)
     scale = 1.0 / math.sqrt(GROUP * rows * parts)

time: 127 us -> 126 us (level)
  blocking collectives: 43.7 us -> 108 us
  waiting for transfers between devices: 45.6 us -> 0.93 us
  starting transfers between devices: 23.6 us -> 4.42 us
    all_to_all x0 -> x1, blocking collectives: none -> 64 us  [on_device(): lax.all_to_all(pack(signal, upstream, long_filter, parts), 'seq', 0, 0, t...]
    all_to_all x1 -> x0, waiting for transfers between devices: 44.1 us -> none  [on_device(): lax.all_to_all(pack(signal, upstream, long_filter, parts), 'seq', 0, 0, t...]
    all_to_all x1 -> x0, starting transfers between devices: 19.3 us -> none  [on_device(): lax.all_to_all(pack(signal, upstream, long_filter, parts), 'seq', 0, 0, t...]
  transfers between devices with their start and end apart: 2 -> 1, of which waited for: 2 -> 1; matrix products, arithmetic and copies ran while one was open for 1% -> 0% of each run, Pallas kernels for 3% -> 4%
where the time goes in v4:
time: 126 us; the launch traced here: 125 us
  blocking collectives  108 us (86%)
  Pallas kernels  11.6 us (9%)
  starting transfers between devices  4.42 us (4%)
    all_to_all x1, blocking collectives, on_device(): lax.all_to_all(pack(signal, upstream, long_filter, parts), 'seq', 0, 0, t...  64 us
    all_to_all x1, blocking collectives, on_device(): lax.all_to_all(stamp(message, short, squares), 'seq', 0, 0, tiled=True)  43.7 us
    pallas_call x1, Pallas kernels, signal_side(): pl.pallas_call(signal_side_kernel, out_shape=(jax.ShapeDtypeStruct((block...  4.43 us
    all_to_all x1, starting transfers between devices, on_device(): squares = lax.all_to_all(squares, 'ch', 0, 0, tiled=True)  4.42 us
    pallas_call x1, Pallas kernels, filter_side(): pl.pallas_call(filter_side_kernel, out_shape=(jax.ShapeDtypeStruct((count...  4.24 us
  transfers between devices with their start and end apart: 1, of which 1 were waited for; matrix products, arithmetic and copies ran while one was open for 0% of the time, Pallas kernels for 4%

profile of v4, /device:TPU:32, one launch (start us, length us, event | category | flops | bytes accessed | tf_op | source)
XLA Modules:
  0.0 125.4 jit_solution(10572928495634100436)
XLA Ops:
  0.6 1.4 %shard_map.103 = bf16[128,24,128]{2,1,0:T(8,128)(2,1)S(1)} custom-call(bf16[128,1024]{1,0:T(8,128)(2,1)} %first_ref.1, bf16[128,1024]{1,0:T(8,128)(2,1)} %second_ref.1, bf16[128,1024]{1,0:T(8,128)(2,1)} %third_ref.1), custom_call_target="tpu_custom_call" | custom-call | flops 1000000 | bytes 1572864 | tf_op jit(solution)/shard_map/pallas_call | solution.py:294
  2.0 0.0 copy-start
  2.0 0.0 copy-start.2
  2.0 0.0 copy-start.3
  2.0 0.0 copy-start.4
  2.0 64.0 %all_to_all.15.got_ref = bf16[128,24,128]{2,1,0:T(8,128)(2,1)S(1)} all-to-all(bf16[128,24,128]{2,1,0:T(8,128)(2,1)S(1)} %shard_map.103), channel_id=1, replica_groups=mesh['seq'=128,'ch'=4] {'seq'}, dimensions={0} | all-to-all | bytes 1572864 | tf_op jit(solution)/shard_map/all_to_all | solution.py:346
  66.0 0.0 copy-done
  66.0 0.0 copy-done.2
  66.0 0.0 copy-done.3
  66.0 0.0 copy-done.4
  66.0 4.2 %shard_map.104 = (f32[1024,256]{1,0:T(8,128)S(1)}, bf16[8,128,128]{2,1,0:T(8,128)(2,1)S(1)}, f32[4,8,128]{2,1,0:T(8,128)}) custom-call(bf16[128,24,128]{2,1,0:T(8,128)(2,1)S(1)} %all_to_all.15.got_ref, bf16[64,128]{1,0:T(8,128)(2,1)S(1)} %bitcast.2, bf16[256,256]{1,0:T(8,128)(2,1)S(1)} %copy-done.4, f32[2,128,128]{2,1,0:T(8,128)S(1)} %copy-done.3, ...), custom_call_target="tpu_custom_call" | custom-call | flops 3000000000 | bytes 6000000 | tf_op jit(solution)/shard_map/pallas_call | solution.py:207
  70.3 0.0 copy-start.1
  70.3 4.4 %all-to-all-start.1 = ((f32[4,8,128]{2,1,0:T(8,128)}), f32[4,8,128]{2,1,0:T(8,128)S(1)}, u32[]{:S(2)}, u32[]{:S(2)}) async-start(f32[4,8,128]{2,1,0:T(8,128)} %get-tuple-element.15), calls=%async_computation.1 | async-start | bytes 32768 | tf_op jit(solution)/shard_map/all_to_all | solution.py:349
  74.7 0.0 copy-done.1
  74.7 4.4 %shard_map.105 = (bf16[128,9,2,128]{3,2,1,0:T(2,128)(2,1)S(1)}, f32[8,128]{1,0:T(8,128)S(1)}) custom-call(bf16[128,24,128]{2,1,0:T(8,128)(2,1)S(1)} %all_to_all.15.got_ref, f32[1024,256]{1,0:T(8,128)S(1)} %get-tuple-element.11.spectrum_ref, bf16[8,128,128]{2,1,0:T(8,128)(2,1)S(1)} %get-tuple-element.12.raw_ref, bf16[64,128]{1,0:T(8,128)(2,1)S(1)} %bitcast.3, ...), custom_call_target="tpu_custom_call" | custom-call | flops 3000000000 | bytes 6000000 | tf_op jit(solution)/shard_map/pallas_call | solution.py:228
  79.1 0.9 all-to-all-done.1.squares_ref
  80.1 0.1 shard_map.106
  80.2 43.7 %all_to_all.16.refs_0_ = bf16[128,9,2,128]{3,2,1,0:T(2,128)(2,1)S(1)} all-to-all(bf16[128,9,2,128]{3,2,1,0:T(2,128)(2,1)S(1)} %shard_map.106), channel_id=1, replica_groups=mesh['seq'=128,'ch'=4] {'seq'}, dimensions={0} | all-to-all | bytes 1179648 | tf_op jit(solution)/shard_map/all_to_all | solution.py:351
  123.9 1.5 %shard_map.107 = (bf16[128,1024]{1,0:T(8,128)(2,1)}, bf16[128,1024]{1,0:T(8,128)(2,1)}, f32[64,128]{1,0:T(8,128)}) custom-call(bf16[128,9,2,128]{3,2,1,0:T(2,128)(2,1)S(1)} %all_to_all.16.refs_0_), custom_call_target="tpu_custom_call" | custom-call | tf_op jit(solution)/shard_map/pallas_call | solution.py:325
Async XLA Ops:
  2.0 64.0 %copy-start = (bf16[128,64]{0,1:T(8,128)(2,1)S(1)}, bf16[128,64]{0,1:T(8,128)(2,1)}, u32[]{:S(2)}) copy-start(bf16[128,64]{0,1:T(8,128)(2,1)} %param.11) | copy-start | bytes 49156
  2.0 64.0 %copy-start.2 = (bf16[2,256,256]{2,1,0:T(8,128)(2,1)S(1)}, bf16[2,256,256]{2,1,0:T(8,128)(2,1)}, u32[]{:S(2)}) copy-start(bf16[2,256,256]{2,1,0:T(8,128)(2,1)} %constant.8.clone.inner_ref) | copy-start | bytes 786436
  2.0 64.0 %copy-start.3 = (f32[2,128,128]{2,1,0:T(8,128)S(1)}, f32[2,128,128]{2,1,0:T(8,128)}, u32[]{:S(2)}) copy-start(f32[2,128,128]{2,1,0:T(8,128)} %constant.7.clone.twist_ref) | copy-start | bytes 393220
  2.0 64.0 %copy-start.4 = (bf16[256,256]{1,0:T(8,128)(2,1)S(1)}, bf16[256,256]{1,0:T(8,128)(2,1)}, u32[]{:S(2)}) copy-start(bf16[256,256]{1,0:T(8,128)(2,1)} %constant.6.clone.enter_ref) | copy-start | bytes 393220
  70.3 4.4 %copy-start.1 = (f32[1024]{0:T(1024)S(1)}, f32[1024]{0:T(1024)}, u32[]{:S(2)}) copy-start(f32[1024]{0:T(1024)} %skip_ref.1) | copy-start | bytes 12292
  70.3 9.8 %all-to-all-start.1 = ((f32[4,8,128]{2,1,0:T(8,128)}), f32[4,8,128]{2,1,0:T(8,128)S(1)}, u32[]{:S(2)}, u32[]{:S(2)}) async-start(f32[4,8,128]{2,1,0:T(8,128)} %get-tuple-element.15), calls=%async_computation.1 | async-start | bytes 32768 | tf_op jit(solution)/shard_map/all_to_all | solution.py:349

commit v5 on v4

--- a/solution.py
+++ b/solution.py
@@ -95,32 +95,41 @@
     return highs, lows
 
 
-def correlate(lefts, rights, enter_ref, twist_ref, inner_ref):
+def correlate(lefts, rights, enter_ref, twist_ref, inner_ref, fine):
     blocks = lefts[0].shape[0]
     width = lefts[0].shape[1] // 2
     twist_real, twist_imag = twist_ref[0], twist_ref[1]
-    highs, lows = [], []
+    transposed = ((1,), (1,))
+    products = []
     for left, right in zip(lefts, rights):
         left_real, left_imag = left[:, :width], left[:, width:]
         real, imag = right[:, :width], right[:, width:]
-        high, low = split(
+        products.append(
             jnp.concatenate(
                 [left_real * real + left_imag * imag, left_imag * real - left_real * imag], axis=1
             )
         )
-        highs.append(high)
-        lows.append(low)
-    backs = three(highs, lows, inner_ref, ((1,), (1,)))
+    if fine:
+        highs, lows = zip(*[split(product) for product in products])
+        backs = three(highs, lows, inner_ref, transposed)
+    else:
+        high = jnp.concatenate([product.astype(BF16) for product in products], axis=0)
+        backs = dot(high, inner_ref[0], transposed)
     reals, imags = [], []
     for n in range(len(lefts)):
         real = backs[n * blocks : (n + 1) * blocks, :width]
         imag = backs[n * blocks : (n + 1) * blocks, width:]
         reals.append(real * twist_real + imag * twist_imag)
         imags.append(imag * twist_real - real * twist_imag)
-    high, low = split(jnp.concatenate([jnp.concatenate(reals, axis=1), jnp.concatenate(imags, axis=1)], axis=0))
+    grid = jnp.concatenate([jnp.concatenate(reals, axis=1), jnp.concatenate(imags, axis=1)], axis=0)
     leave = enter_ref[...].T
-    wide = dot(leave, high)
-    return (wide[:blocks] + (wide[blocks:] + dot(leave[:blocks], low))) * (1.0 / (blocks * width))
+    if fine:
+        high, low = split(grid)
+        wide = dot(leave, high)
+        result = wide[:blocks] + (wide[blocks:] + dot(leave[:blocks], low))
+    else:
+        result = dot(leave[:blocks], grid.astype(BF16))
+    return result * (1.0 / (blocks * width))
 
 
 def filter_side_kernel(
@@ -147,7 +156,7 @@
     spectrum_ref[...] = spectra[: count * blocks]
     lefts = [spectra[c * blocks : (c + 1) * blocks] for c in range(count)]
     rights = [spectra[(count + c) * blocks : (count + c + 1) * blocks] for c in range(count)]
-    result = correlate(lefts, rights, enter_ref, twist_ref, inner_ref)
+    result = correlate(lefts, rights, enter_ref, twist_ref, inner_ref, False)
     squares = jnp.zeros((blocks, width), F32)
     for c in range(count):
         raw = result[:, c * width : (c + 1) * width].astype(BF16)
@@ -173,7 +182,7 @@
     spectra = three(highs, lows, inner_ref)
     lefts = [spectrum_ref[c * blocks : (c + 1) * blocks, :] for c in range(count)]
     rights = [spectra[c * blocks : (c + 1) * blocks] for c in range(count)]
-    result = correlate(lefts, rights, enter_ref, twist_ref, inner_ref)
+    result = correlate(lefts, rights, enter_ref, twist_ref, inner_ref, True)
     first = lax.axis_index("seq") * count
     pairs, grads, signals = [], [], []
     for c in range(count):

time: 126 us -> 125 us (level)
  no operation moved by 1% of the time
where the time goes in v5:
time: 125 us; the launch traced here: 124 us
  blocking collectives  108 us (86%)
  Pallas kernels  10.5 us (8%)
  starting transfers between devices  4.42 us (4%)
    all_to_all x1, blocking collectives, on_device(): lax.all_to_all(pack(signal, upstream, long_filter, parts), 'seq', 0, 0, t...  64 us
    all_to_all x1, blocking collectives, on_device(): lax.all_to_all(stamp(message, short, squares), 'seq', 0, 0, tiled=True)  43.7 us
    all_to_all x1, starting transfers between devices, on_device(): squares = lax.all_to_all(squares, 'ch', 0, 0, tiled=True)  4.42 us
    pallas_call x1, Pallas kernels, signal_side(): pl.pallas_call(signal_side_kernel, out_shape=(jax.ShapeDtypeStruct((block...  4.42 us
    pallas_call x1, Pallas kernels, filter_side(): pl.pallas_call(filter_side_kernel, out_shape=(jax.ShapeDtypeStruct((count...  3.14 us
  transfers between devices with their start and end apart: 1, of which 1 were waited for; matrix products, arithmetic and copies ran while one was open for 0% of the time, Pallas kernels for 4%

profile of v5, /device:TPU:32, one launch (start us, length us, event | category | flops | bytes accessed | tf_op | source)
XLA Modules:
  0.0 124.3 jit_solution(4798717391440708841)
XLA Ops:
  0.6 1.4 %shard_map.103 = bf16[128,24,128]{2,1,0:T(8,128)(2,1)S(1)} custom-call(bf16[128,1024]{1,0:T(8,128)(2,1)} %first_ref.1, bf16[128,1024]{1,0:T(8,128)(2,1)} %second_ref.1, bf16[128,1024]{1,0:T(8,128)(2,1)} %third_ref.1), custom_call_target="tpu_custom_call" | custom-call | flops 1000000 | bytes 1572864 | tf_op jit(solution)/shard_map/pallas_call | solution.py:303
  2.0 0.0 copy-start
  2.0 0.0 copy-start.2
  2.0 0.0 copy-start.3
  2.0 0.0 copy-start.4
  2.0 64.0 %all_to_all.15.got_ref = bf16[128,24,128]{2,1,0:T(8,128)(2,1)S(1)} all-to-all(bf16[128,24,128]{2,1,0:T(8,128)(2,1)S(1)} %shard_map.103), channel_id=1, replica_groups=mesh['seq'=128,'ch'=4] {'seq'}, dimensions={0} | all-to-all | bytes 1572864 | tf_op jit(solution)/shard_map/all_to_all | solution.py:355
  66.0 0.0 copy-done
  66.0 0.0 copy-done.2
  66.0 0.0 copy-done.3
  66.0 0.0 copy-done.4
  66.0 3.1 %shard_map.104 = (f32[1024,256]{1,0:T(8,128)S(1)}, bf16[8,128,128]{2,1,0:T(8,128)(2,1)S(1)}, f32[4,8,128]{2,1,0:T(8,128)}) custom-call(bf16[128,24,128]{2,1,0:T(8,128)(2,1)S(1)} %all_to_all.15.got_ref, bf16[64,128]{1,0:T(8,128)(2,1)S(1)} %bitcast.2, bf16[256,256]{1,0:T(8,128)(2,1)S(1)} %copy-done.4, f32[2,128,128]{2,1,0:T(8,128)S(1)} %copy-done.3, ...), custom_call_target="tpu_custom_call" | custom-call | flops 3000000000 | bytes 6000000 | tf_op jit(solution)/shard_map/pallas_call | solution.py:216
  69.2 0.0 copy-start.1
  69.2 4.4 %all-to-all-start.1 = ((f32[4,8,128]{2,1,0:T(8,128)}), f32[4,8,128]{2,1,0:T(8,128)S(1)}, u32[]{:S(2)}, u32[]{:S(2)}) async-start(f32[4,8,128]{2,1,0:T(8,128)} %get-tuple-element.15), calls=%async_computation.1 | async-start | bytes 32768 | tf_op jit(solution)/shard_map/all_to_all | solution.py:358
  73.6 0.0 copy-done.1
  73.6 4.4 %shard_map.105 = (bf16[128,9,2,128]{3,2,1,0:T(2,128)(2,1)S(1)}, f32[8,128]{1,0:T(8,128)S(1)}) custom-call(bf16[128,24,128]{2,1,0:T(8,128)(2,1)S(1)} %all_to_all.15.got_ref, f32[1024,256]{1,0:T(8,128)S(1)} %get-tuple-element.11.spectrum_ref, bf16[8,128,128]{2,1,0:T(8,128)(2,1)S(1)} %get-tuple-element.12.raw_ref, bf16[64,128]{1,0:T(8,128)(2,1)S(1)} %bitcast.3, ...), custom_call_target="tpu_custom_call" | custom-call | flops 3000000000 | bytes 6000000 | tf_op jit(solution)/shard_map/pallas_call | solution.py:237
  78.0 0.9 all-to-all-done.1.squares_ref
  79.0 0.1 shard_map.106
  79.1 43.7 %all_to_all.16.refs_0_ = bf16[128,9,2,128]{3,2,1,0:T(2,128)(2,1)S(1)} all-to-all(bf16[128,9,2,128]{3,2,1,0:T(2,128)(2,1)S(1)} %shard_map.106), channel_id=1, replica_groups=mesh['seq'=128,'ch'=4] {'seq'}, dimensions={0} | all-to-all | bytes 1179648 | tf_op jit(solution)/shard_map/all_to_all | solution.py:360
  122.8 1.5 %shard_map.107 = (bf16[128,1024]{1,0:T(8,128)(2,1)}, bf16[128,1024]{1,0:T(8,128)(2,1)}, f32[64,128]{1,0:T(8,128)}) custom-call(bf16[128,9,2,128]{3,2,1,0:T(2,128)(2,1)S(1)} %all_to_all.16.refs_0_), custom_call_target="tpu_custom_call" | custom-call | tf_op jit(solution)/shard_map/pallas_call | solution.py:334
Async XLA Ops:
  2.0 64.0 %copy-start = (bf16[128,64]{0,1:T(8,128)(2,1)S(1)}, bf16[128,64]{0,1:T(8,128)(2,1)}, u32[]{:S(2)}) copy-start(bf16[128,64]{0,1:T(8,128)(2,1)} %param.11) | copy-start | bytes 49156
  2.0 64.0 %copy-start.2 = (bf16[2,256,256]{2,1,0:T(8,128)(2,1)S(1)}, bf16[2,256,256]{2,1,0:T(8,128)(2,1)}, u32[]{:S(2)}) copy-start(bf16[2,256,256]{2,1,0:T(8,128)(2,1)} %constant.8.clone.inner_ref) | copy-start | bytes 786436
  2.0 64.0 %copy-start.3 = (f32[2,128,128]{2,1,0:T(8,128)S(1)}, f32[2,128,128]{2,1,0:T(8,128)}, u32[]{:S(2)}) copy-start(f32[2,128,128]{2,1,0:T(8,128)} %constant.7.clone.twist_ref) | copy-start | bytes 393220
  2.0 64.0 %copy-start.4 = (bf16[256,256]{1,0:T(8,128)(2,1)S(1)}, bf16[256,256]{1,0:T(8,128)(2,1)}, u32[]{:S(2)}) copy-start(bf16[256,256]{1,0:T(8,128)(2,1)} %constant.6.clone.enter_ref) | copy-start | bytes 393220
  69.2 4.4 %copy-start.1 = (f32[1024]{0:T(1024)S(1)}, f32[1024]{0:T(1024)}, u32[]{:S(2)}) copy-start(f32[1024]{0:T(1024)} %skip_ref.1) | copy-start | bytes 12292
  69.2 9.8 %all-to-all-start.1 = ((f32[4,8,128]{2,1,0:T(8,128)}), f32[4,8,128]{2,1,0:T(8,128)S(1)}, u32[]{:S(2)}, u32[]{:S(2)}) async-start(f32[4,8,128]{2,1,0:T(8,128)} %get-tuple-element.15), calls=%async_computation.1 | async-start | bytes 32768 | tf_op jit(solution)/shard_map/all_to_all | solution.py:358

commit v6 on v5

--- a/solution.py
+++ b/solution.py
@@ -150,12 +150,14 @@
         pairs.append(jnp.concatenate([before, signal], axis=1).astype(BF16))
         columns.append(channel_rows(rows_ref, count + c, lanes_here, blocks).astype(BF16))
     mixed = dot(jnp.concatenate(pairs, axis=0), mix_table).astype(BF16)
-    columns += [mixed[c * blocks : (c + 1) * blocks] for c in range(count)]
     highs, lows = enter_grid(columns, enter_ref, twist_ref)
-    spectra = three(highs, lows, inner_ref)
-    spectrum_ref[...] = spectra[: count * blocks]
-    lefts = [spectra[c * blocks : (c + 1) * blocks] for c in range(count)]
-    rights = [spectra[(count + c) * blocks : (count + c + 1) * blocks] for c in range(count)]
+    upstreams = three(highs, lows, inner_ref)
+    spectrum_ref[...] = upstreams
+    columns = [mixed[c * blocks : (c + 1) * blocks] for c in range(count)]
+    highs, lows = enter_grid(columns, enter_ref, twist_ref)
+    mixeds = three(highs, lows, inner_ref)
+    lefts = [upstreams[c * blocks : (c + 1) * blocks] for c in range(count)]
+    rights = [mixeds[c * blocks : (c + 1) * blocks] for c in range(count)]
     result = correlate(lefts, rights, enter_ref, twist_ref, inner_ref, False)
     squares = jnp.zeros((blocks, width), F32)
     for c in range(count):

time: 125 us -> 124 us (level)
  no operation moved by 1% of the time
where the time goes in v6:
time: 124 us
  blocking collectives  108 us (87%)
  Pallas kernels  10.2 us (8%)
  starting transfers between devices  4.42 us (4%)
    all_to_all x1, blocking collectives, on_device(): lax.all_to_all(pack(signal, upstream, long_filter, parts), 'seq', 0, 0, t...  64 us
    all_to_all x1, blocking collectives, on_device(): lax.all_to_all(stamp(message, short, squares), 'seq', 0, 0, tiled=True)  43.7 us
    pallas_call x1, Pallas kernels, signal_side(): pl.pallas_call(signal_side_kernel, out_shape=(jax.ShapeDtypeStruct((block...  4.42 us
    all_to_all x1, starting transfers between devices, on_device(): squares = lax.all_to_all(squares, 'ch', 0, 0, tiled=True)  4.42 us
    pallas_call x1, Pallas kernels, filter_side(): pl.pallas_call(filter_side_kernel, out_shape=(jax.ShapeDtypeStruct((count...  2.9 us
  transfers between devices with their start and end apart: 1, of which 1 were waited for; matrix products, arithmetic and copies ran while one was open for 0% of the time, Pallas kernels for 4%

profile of v6, /device:TPU:32, one launch (start us, length us, event | category | flops | bytes accessed | tf_op | source)
XLA Modules:
  0.0 124.0 jit_solution(5258519563078669225)
XLA Ops:
  0.6 1.4 %shard_map.103 = bf16[128,24,128]{2,1,0:T(8,128)(2,1)S(1)} custom-call(bf16[128,1024]{1,0:T(8,128)(2,1)} %first_ref.1, bf16[128,1024]{1,0:T(8,128)(2,1)} %second_ref.1, bf16[128,1024]{1,0:T(8,128)(2,1)} %third_ref.1), custom_call_target="tpu_custom_call" | custom-call | flops 1000000 | bytes 1572864 | tf_op jit(solution)/shard_map/pallas_call | solution.py:305
  2.0 0.0 copy-start
  2.0 0.0 copy-start.2
  2.0 0.0 copy-start.3
  2.0 0.0 copy-start.4
  2.0 64.0 %all_to_all.15.got_ref = bf16[128,24,128]{2,1,0:T(8,128)(2,1)S(1)} all-to-all(bf16[128,24,128]{2,1,0:T(8,128)(2,1)S(1)} %shard_map.103), channel_id=1, replica_groups=mesh['seq'=128,'ch'=4] {'seq'}, dimensions={0} | all-to-all | bytes 1572864 | tf_op jit(solution)/shard_map/all_to_all | solution.py:357
  66.0 0.0 copy-done
  66.0 0.0 copy-done.2
  66.0 0.0 copy-done.3
  66.0 0.0 copy-done.4
  66.0 2.9 %shard_map.104 = (f32[1024,256]{1,0:T(8,128)S(1)}, bf16[8,128,128]{2,1,0:T(8,128)(2,1)S(1)}, f32[4,8,128]{2,1,0:T(8,128)}) custom-call(bf16[128,24,128]{2,1,0:T(8,128)(2,1)S(1)} %all_to_all.15.got_ref, bf16[64,128]{1,0:T(8,128)(2,1)S(1)} %bitcast.2, bf16[256,256]{1,0:T(8,128)(2,1)S(1)} %copy-done.4, f32[2,128,128]{2,1,0:T(8,128)S(1)} %copy-done.3, ...), custom_call_target="tpu_custom_call" | custom-call | flops 3000000000 | bytes 6000000 | tf_op jit(solution)/shard_map/pallas_call | solution.py:218
  68.9 0.0 copy-start.1
  68.9 4.4 %all-to-all-start.1 = ((f32[4,8,128]{2,1,0:T(8,128)}), f32[4,8,128]{2,1,0:T(8,128)S(1)}, u32[]{:S(2)}, u32[]{:S(2)}) async-start(f32[4,8,128]{2,1,0:T(8,128)} %get-tuple-element.15), calls=%async_computation.1 | async-start | bytes 32768 | tf_op jit(solution)/shard_map/all_to_all | solution.py:360
  73.4 0.0 copy-done.1
  73.4 4.4 %shard_map.105 = (bf16[128,9,2,128]{3,2,1,0:T(2,128)(2,1)S(1)}, f32[8,128]{1,0:T(8,128)S(1)}) custom-call(bf16[128,24,128]{2,1,0:T(8,128)(2,1)S(1)} %all_to_all.15.got_ref, f32[1024,256]{1,0:T(8,128)S(1)} %get-tuple-element.11.spectrum_ref, bf16[8,128,128]{2,1,0:T(8,128)(2,1)S(1)} %get-tuple-element.12.raw_ref, bf16[64,128]{1,0:T(8,128)(2,1)S(1)} %bitcast.3, ...), custom_call_target="tpu_custom_call" | custom-call | flops 3000000000 | bytes 6000000 | tf_op jit(solution)/shard_map/pallas_call | solution.py:239
  77.8 0.9 all-to-all-done.1.squares_ref
  78.7 0.1 shard_map.106
  78.8 43.7 %all_to_all.16.refs_0_ = bf16[128,9,2,128]{3,2,1,0:T(2,128)(2,1)S(1)} all-to-all(bf16[128,9,2,128]{3,2,1,0:T(2,128)(2,1)S(1)} %shard_map.106), channel_id=1, replica_groups=mesh['seq'=128,'ch'=4] {'seq'}, dimensions={0} | all-to-all | bytes 1179648 | tf_op jit(solution)/shard_map/all_to_all | solution.py:362
  122.6 1.5 %shard_map.107 = (bf16[128,1024]{1,0:T(8,128)(2,1)}, bf16[128,1024]{1,0:T(8,128)(2,1)}, f32[64,128]{1,0:T(8,128)}) custom-call(bf16[128,9,2,128]{3,2,1,0:T(2,128)(2,1)S(1)} %all_to_all.16.refs_0_), custom_call_target="tpu_custom_call" | custom-call | tf_op jit(solution)/shard_map/pallas_call | solution.py:336
Async XLA Ops:
  2.0 64.0 %copy-start = (bf16[128,64]{0,1:T(8,128)(2,1)S(1)}, bf16[128,64]{0,1:T(8,128)(2,1)}, u32[]{:S(2)}) copy-start(bf16[128,64]{0,1:T(8,128)(2,1)} %param.11) | copy-start | bytes 49156
  2.0 64.0 %copy-start.2 = (bf16[2,256,256]{2,1,0:T(8,128)(2,1)S(1)}, bf16[2,256,256]{2,1,0:T(8,128)(2,1)}, u32[]{:S(2)}) copy-start(bf16[2,256,256]{2,1,0:T(8,128)(2,1)} %constant.8.clone.inner_ref) | copy-start | bytes 786436
  2.0 64.0 %copy-start.3 = (f32[2,128,128]{2,1,0:T(8,128)S(1)}, f32[2,128,128]{2,1,0:T(8,128)}, u32[]{:S(2)}) copy-start(f32[2,128,128]{2,1,0:T(8,128)} %constant.7.clone.twist_ref) | copy-start | bytes 393220
  2.0 64.0 %copy-start.4 = (bf16[256,256]{1,0:T(8,128)(2,1)S(1)}, bf16[256,256]{1,0:T(8,128)(2,1)}, u32[]{:S(2)}) copy-start(bf16[256,256]{1,0:T(8,128)(2,1)} %constant.6.clone.enter_ref) | copy-start | bytes 393220
  68.9 4.4 %copy-start.1 = (f32[1024]{0:T(1024)S(1)}, f32[1024]{0:T(1024)}, u32[]{:S(2)}) copy-start(f32[1024]{0:T(1024)} %skip_ref.1) | copy-start | bytes 12292
  68.9 9.8 %all-to-all-start.1 = ((f32[4,8,128]{2,1,0:T(8,128)}), f32[4,8,128]{2,1,0:T(8,128)S(1)}, u32[]{:S(2)}, u32[]{:S(2)}) async-start(f32[4,8,128]{2,1,0:T(8,128)} %get-tuple-element.15), calls=%async_computation.1 | async-start | bytes 32768 | tf_op jit(solution)/shard_map/all_to_all | solution.py:360

commit v7 on v6

--- a/solution.py
+++ b/solution.py
@@ -220,7 +220,7 @@
         out_shape=(
             jax.ShapeDtypeStruct((count * blocks, 2 * width), F32),
             jax.ShapeDtypeStruct((count, blocks, width), BF16),
-            jax.ShapeDtypeStruct((slabs, 8, width), F32),
+            jax.ShapeDtypeStruct((slabs, 1, width), F32),
         ),
         in_specs=[vmem] * 5,
         out_specs=(vmem,) * 3,

time: 124 us -> 124 us (level)
  no operation moved by 1% of the time
where the time goes in v7:
time: 124 us
  blocking collectives  108 us (87%)
  Pallas kernels  10.2 us (8%)
  starting transfers between devices  4.43 us (4%)
    all_to_all x1, blocking collectives, on_device(): lax.all_to_all(pack(signal, upstream, long_filter, parts), 'seq', 0, 0, t...  64 us
    all_to_all x1, blocking collectives, on_device(): lax.all_to_all(stamp(message, short, squares), 'seq', 0, 0, tiled=True)  43.7 us
    all_to_all x1, starting transfers between devices, on_device(): squares = lax.all_to_all(squares, 'ch', 0, 0, tiled=True)  4.43 us
    pallas_call x1, Pallas kernels, signal_side(): pl.pallas_call(signal_side_kernel, out_shape=(jax.ShapeDtypeStruct((block...  4.42 us
    pallas_call x1, Pallas kernels, filter_side(): pl.pallas_call(filter_side_kernel, out_shape=(jax.ShapeDtypeStruct((count...  2.88 us
  transfers between devices with their start and end apart: 1, of which 1 were waited for; matrix products, arithmetic and copies ran while one was open for 0% of the time, Pallas kernels for 4%

profile of v7, /device:TPU:32, one launch (start us, length us, event | category | flops | bytes accessed | tf_op | source)
XLA Modules:
  0.0 123.8 jit_solution(1725397304825496698)
XLA Ops:
  0.6 1.4 %shard_map.103 = bf16[128,24,128]{2,1,0:T(8,128)(2,1)S(1)} custom-call(bf16[128,1024]{1,0:T(8,128)(2,1)} %first_ref.1, bf16[128,1024]{1,0:T(8,128)(2,1)} %second_ref.1, bf16[128,1024]{1,0:T(8,128)(2,1)} %third_ref.1), custom_call_target="tpu_custom_call" | custom-call | flops 1000000 | bytes 1572864 | tf_op jit(solution)/shard_map/pallas_call | solution.py:305
  2.0 0.0 copy-start
  2.0 0.0 copy-start.2
  2.0 0.0 copy-start.3
  2.0 0.0 copy-start.4
  2.0 64.0 %all_to_all.15.got_ref = bf16[128,24,128]{2,1,0:T(8,128)(2,1)S(1)} all-to-all(bf16[128,24,128]{2,1,0:T(8,128)(2,1)S(1)} %shard_map.103), channel_id=1, replica_groups=mesh['seq'=128,'ch'=4] {'seq'}, dimensions={0} | all-to-all | bytes 1572864 | tf_op jit(solution)/shard_map/all_to_all | solution.py:357
  66.0 0.0 copy-done
  66.0 0.0 copy-done.2
  66.0 0.0 copy-done.3
  66.0 0.0 copy-done.4
  66.0 2.9 %shard_map.104 = (f32[1024,256]{1,0:T(8,128)S(1)}, bf16[8,128,128]{2,1,0:T(8,128)(2,1)S(1)}, f32[4,1,128]{2,1,0:T(1,128)}) custom-call(bf16[128,24,128]{2,1,0:T(8,128)(2,1)S(1)} %all_to_all.15.got_ref, bf16[64,128]{1,0:T(8,128)(2,1)S(1)} %bitcast.2, bf16[256,256]{1,0:T(8,128)(2,1)S(1)} %copy-done.4, f32[2,128,128]{2,1,0:T(8,128)S(1)} %copy-done.3, ...), custom_call_target="tpu_custom_call" | custom-call | flops 3000000000 | bytes 6000000 | tf_op jit(solution)/shard_map/pallas_call | solution.py:218
  68.9 0.0 copy-start.1
  68.9 4.4 %all-to-all-start.1 = ((f32[4,1,128]{2,1,0:T(1,128)}), f32[4,1,128]{2,1,0:T(1,128)S(1)}, u32[]{:S(2)}, u32[]{:S(2)}) async-start(f32[4,1,128]{2,1,0:T(1,128)} %get-tuple-element.15), calls=%async_computation.1 | async-start | bytes 4096 | tf_op jit(solution)/shard_map/all_to_all | solution.py:360
  73.3 0.0 copy-done.1
  73.3 4.4 %shard_map.105 = (bf16[128,9,2,128]{3,2,1,0:T(2,128)(2,1)S(1)}, f32[8,128]{1,0:T(8,128)S(1)}) custom-call(bf16[128,24,128]{2,1,0:T(8,128)(2,1)S(1)} %all_to_all.15.got_ref, f32[1024,256]{1,0:T(8,128)S(1)} %get-tuple-element.11.spectrum_ref, bf16[8,128,128]{2,1,0:T(8,128)(2,1)S(1)} %get-tuple-element.12.raw_ref, bf16[64,128]{1,0:T(8,128)(2,1)S(1)} %bitcast.3, ...), custom_call_target="tpu_custom_call" | custom-call | flops 3000000000 | bytes 6000000 | tf_op jit(solution)/shard_map/pallas_call | solution.py:239
  77.8 0.8 all-to-all-done.1.squares_ref
  78.5 0.1 shard_map.106
  78.6 43.7 %all_to_all.16.refs_0_ = bf16[128,9,2,128]{3,2,1,0:T(2,128)(2,1)S(1)} all-to-all(bf16[128,9,2,128]{3,2,1,0:T(2,128)(2,1)S(1)} %shard_map.106), channel_id=1, replica_groups=mesh['seq'=128,'ch'=4] {'seq'}, dimensions={0} | all-to-all | bytes 1179648 | tf_op jit(solution)/shard_map/all_to_all | solution.py:362
  122.4 1.5 %shard_map.107 = (bf16[128,1024]{1,0:T(8,128)(2,1)}, bf16[128,1024]{1,0:T(8,128)(2,1)}, f32[64,128]{1,0:T(8,128)}) custom-call(bf16[128,9,2,128]{3,2,1,0:T(2,128)(2,1)S(1)} %all_to_all.16.refs_0_), custom_call_target="tpu_custom_call" | custom-call | tf_op jit(solution)/shard_map/pallas_call | solution.py:336
Async XLA Ops:
  2.0 64.0 %copy-start = (bf16[128,64]{0,1:T(8,128)(2,1)S(1)}, bf16[128,64]{0,1:T(8,128)(2,1)}, u32[]{:S(2)}) copy-start(bf16[128,64]{0,1:T(8,128)(2,1)} %param.11) | copy-start | bytes 49156
  2.0 64.0 %copy-start.2 = (bf16[2,256,256]{2,1,0:T(8,128)(2,1)S(1)}, bf16[2,256,256]{2,1,0:T(8,128)(2,1)}, u32[]{:S(2)}) copy-start(bf16[2,256,256]{2,1,0:T(8,128)(2,1)} %constant.8.clone.inner_ref) | copy-start | bytes 786436
  2.0 64.0 %copy-start.3 = (f32[2,128,128]{2,1,0:T(8,128)S(1)}, f32[2,128,128]{2,1,0:T(8,128)}, u32[]{:S(2)}) copy-start(f32[2,128,128]{2,1,0:T(8,128)} %constant.7.clone.twist_ref) | copy-start | bytes 393220
  2.0 64.0 %copy-start.4 = (bf16[256,256]{1,0:T(8,128)(2,1)S(1)}, bf16[256,256]{1,0:T(8,128)(2,1)}, u32[]{:S(2)}) copy-start(bf16[256,256]{1,0:T(8,128)(2,1)} %constant.6.clone.enter_ref) | copy-start | bytes 393220
  68.9 4.4 %copy-start.1 = (f32[1024]{0:T(1024)S(1)}, f32[1024]{0:T(1024)}, u32[]{:S(2)}) copy-start(f32[1024]{0:T(1024)} %skip_ref.1) | copy-start | bytes 12292
  68.9 9.6 %all-to-all-start.1 = ((f32[4,1,128]{2,1,0:T(1,128)}), f32[4,1,128]{2,1,0:T(1,128)S(1)}, u32[]{:S(2)}, u32[]{:S(2)}) async-start(f32[4,1,128]{2,1,0:T(1,128)} %get-tuple-element.15), calls=%async_computation.1 | async-start | bytes 4096 | tf_op jit(solution)/shard_map/all_to_all | solution.py:360

commit v8 on v7

--- a/solution.py
+++ b/solution.py
@@ -325,9 +325,9 @@
     short_ref[...] = jnp.sum(short.reshape(groups, parts // groups, rows), axis=1) * scale
     squares = jnp.sum(jnp.where(lane < 2, low, 0.0), axis=(0, 1), keepdims=True)
     divisor = jnp.maximum(1.0, jnp.sqrt(squares * (1.0 / entries)))
-    signal_ref[...] = back_ref[:, half : 2 * half].astype(F32).reshape(channels, rows).T.astype(BF16)
+    signal_ref[...] = back_ref[:, half : 2 * half].reshape(channels, rows).T
     raw = back_ref[:, :half].astype(F32).reshape(channels, rows)
-    filter_ref[...] = (raw / divisor).T.astype(BF16)
+    filter_ref[...] = (raw / divisor).astype(BF16).T
 
 
 def finish(back, channels, groups, entries, scale):

time: 124 us -> 124 us (level)
  no operation moved by 1% of the time
where the time goes in v8:
time: 124 us
  blocking collectives  108 us (87%)
  Pallas kernels  10.1 us (8%)
  starting transfers between devices  4.43 us (4%)
    all_to_all x1, blocking collectives, on_device(): lax.all_to_all(pack(signal, upstream, long_filter, parts), 'seq', 0, 0, t...  64 us
    all_to_all x1, blocking collectives, on_device(): lax.all_to_all(stamp(message, short, squares), 'seq', 0, 0, tiled=True)  43.7 us
    all_to_all x1, starting transfers between devices, on_device(): squares = lax.all_to_all(squares, 'ch', 0, 0, tiled=True)  4.43 us
    pallas_call x1, Pallas kernels, signal_side(): pl.pallas_call(signal_side_kernel, out_shape=(jax.ShapeDtypeStruct((block...  4.42 us
    pallas_call x1, Pallas kernels, filter_side(): pl.pallas_call(filter_side_kernel, out_shape=(jax.ShapeDtypeStruct((count...  2.88 us
  transfers between devices with their start and end apart: 1, of which 1 were waited for; matrix products, arithmetic and copies ran while one was open for 0% of the time, Pallas kernels for 4%

profile of v8, /device:TPU:32, one launch (start us, length us, event | category | flops | bytes accessed | tf_op | source)
XLA Modules:
  0.0 123.7 jit_solution(2942069631473803868)
XLA Ops:
  0.6 1.4 %shard_map.103 = bf16[128,24,128]{2,1,0:T(8,128)(2,1)S(1)} custom-call(bf16[128,1024]{1,0:T(8,128)(2,1)} %first_ref.1, bf16[128,1024]{1,0:T(8,128)(2,1)} %second_ref.1, bf16[128,1024]{1,0:T(8,128)(2,1)} %third_ref.1), custom_call_target="tpu_custom_call" | custom-call | flops 1000000 | bytes 1572864 | tf_op jit(solution)/shard_map/pallas_call | solution.py:305
  2.0 0.0 copy-start
  2.0 0.0 copy-start.2
  2.0 0.0 copy-start.3
  2.0 0.0 copy-start.4
  2.0 64.0 %all_to_all.15.got_ref = bf16[128,24,128]{2,1,0:T(8,128)(2,1)S(1)} all-to-all(bf16[128,24,128]{2,1,0:T(8,128)(2,1)S(1)} %shard_map.103), channel_id=1, replica_groups=mesh['seq'=128,'ch'=4] {'seq'}, dimensions={0} | all-to-all | bytes 1572864 | tf_op jit(solution)/shard_map/all_to_all | solution.py:357
  66.0 0.0 copy-done
  66.0 0.0 copy-done.2
  66.0 0.0 copy-done.3
  66.0 0.0 copy-done.4
  66.0 2.9 %shard_map.104 = (f32[1024,256]{1,0:T(8,128)S(1)}, bf16[8,128,128]{2,1,0:T(8,128)(2,1)S(1)}, f32[4,1,128]{2,1,0:T(1,128)}) custom-call(bf16[128,24,128]{2,1,0:T(8,128)(2,1)S(1)} %all_to_all.15.got_ref, bf16[64,128]{1,0:T(8,128)(2,1)S(1)} %bitcast.2, bf16[256,256]{1,0:T(8,128)(2,1)S(1)} %copy-done.4, f32[2,128,128]{2,1,0:T(8,128)S(1)} %copy-done.3, ...), custom_call_target="tpu_custom_call" | custom-call | flops 3000000000 | bytes 6000000 | tf_op jit(solution)/shard_map/pallas_call | solution.py:218
  68.9 0.0 copy-start.1
  68.9 4.4 %all-to-all-start.1 = ((f32[4,1,128]{2,1,0:T(1,128)}), f32[4,1,128]{2,1,0:T(1,128)S(1)}, u32[]{:S(2)}, u32[]{:S(2)}) async-start(f32[4,1,128]{2,1,0:T(1,128)} %get-tuple-element.15), calls=%async_computation.1 | async-start | bytes 4096 | tf_op jit(solution)/shard_map/all_to_all | solution.py:360
  73.3 0.0 copy-done.1
  73.3 4.4 %shard_map.105 = (bf16[128,9,2,128]{3,2,1,0:T(2,128)(2,1)S(1)}, f32[8,128]{1,0:T(8,128)S(1)}) custom-call(bf16[128,24,128]{2,1,0:T(8,128)(2,1)S(1)} %all_to_all.15.got_ref, f32[1024,256]{1,0:T(8,128)S(1)} %get-tuple-element.11.spectrum_ref, bf16[8,128,128]{2,1,0:T(8,128)(2,1)S(1)} %get-tuple-element.12.raw_ref, bf16[64,128]{1,0:T(8,128)(2,1)S(1)} %bitcast.3, ...), custom_call_target="tpu_custom_call" | custom-call | flops 3000000000 | bytes 6000000 | tf_op jit(solution)/shard_map/pallas_call | solution.py:239
  77.8 0.8 all-to-all-done.1.squares_ref
  78.5 0.1 shard_map.106
  78.6 43.7 %all_to_all.16.refs_0_ = bf16[128,9,2,128]{3,2,1,0:T(2,128)(2,1)S(1)} all-to-all(bf16[128,9,2,128]{3,2,1,0:T(2,128)(2,1)S(1)} %shard_map.106), channel_id=1, replica_groups=mesh['seq'=128,'ch'=4] {'seq'}, dimensions={0} | all-to-all | bytes 1179648 | tf_op jit(solution)/shard_map/all_to_all | solution.py:362
  122.4 1.4 %shard_map.107 = (bf16[128,1024]{1,0:T(8,128)(2,1)}, bf16[128,1024]{1,0:T(8,128)(2,1)}, f32[64,128]{1,0:T(8,128)}) custom-call(bf16[128,9,2,128]{3,2,1,0:T(2,128)(2,1)S(1)} %all_to_all.16.refs_0_), custom_call_target="tpu_custom_call" | custom-call | tf_op jit(solution)/shard_map/pallas_call | solution.py:336
Async XLA Ops:
  2.0 64.0 %copy-start = (bf16[128,64]{0,1:T(8,128)(2,1)S(1)}, bf16[128,64]{0,1:T(8,128)(2,1)}, u32[]{:S(2)}) copy-start(bf16[128,64]{0,1:T(8,128)(2,1)} %param.11) | copy-start | bytes 49156
  2.0 64.0 %copy-start.2 = (bf16[2,256,256]{2,1,0:T(8,128)(2,1)S(1)}, bf16[2,256,256]{2,1,0:T(8,128)(2,1)}, u32[]{:S(2)}) copy-start(bf16[2,256,256]{2,1,0:T(8,128)(2,1)} %constant.8.clone.inner_ref) | copy-start | bytes 786436
  2.0 64.0 %copy-start.3 = (f32[2,128,128]{2,1,0:T(8,128)S(1)}, f32[2,128,128]{2,1,0:T(8,128)}, u32[]{:S(2)}) copy-start(f32[2,128,128]{2,1,0:T(8,128)} %constant.7.clone.twist_ref) | copy-start | bytes 393220
  2.0 64.0 %copy-start.4 = (bf16[256,256]{1,0:T(8,128)(2,1)S(1)}, bf16[256,256]{1,0:T(8,128)(2,1)}, u32[]{:S(2)}) copy-start(bf16[256,256]{1,0:T(8,128)(2,1)} %constant.6.clone.enter_ref) | copy-start | bytes 393220
  68.9 4.4 %copy-start.1 = (f32[1024]{0:T(1024)S(1)}, f32[1024]{0:T(1024)}, u32[]{:S(2)}) copy-start(f32[1024]{0:T(1024)} %skip_ref.1) | copy-start | bytes 12292
  68.9 9.6 %all-to-all-start.1 = ((f32[4,1,128]{2,1,0:T(1,128)}), f32[4,1,128]{2,1,0:T(1,128)S(1)}, u32[]{:S(2)}, u32[]{:S(2)}) async-start(f32[4,1,128]{2,1,0:T(1,128)} %get-tuple-element.15), calls=%async_computation.1 | async-start | bytes 4096 | tf_op jit(solution)/shard_map/all_to_all | solution.py:360

commit v9 on v8

--- a/solution.py
+++ b/solution.py
@@ -122,13 +122,13 @@
         reals.append(real * twist_real + imag * twist_imag)
         imags.append(imag * twist_real - real * twist_imag)
     grid = jnp.concatenate([jnp.concatenate(reals, axis=1), jnp.concatenate(imags, axis=1)], axis=0)
-    leave = enter_ref[...].T
     if fine:
+        leave = enter_ref[...].T
         high, low = split(grid)
         wide = dot(leave, high)
         result = wide[:blocks] + (wide[blocks:] + dot(leave[:blocks], low))
     else:
-        result = dot(leave[:blocks], grid.astype(BF16))
+        result = dot(enter_ref[:, :blocks].T, grid.astype(BF16))
     return result * (1.0 / (blocks * width))
 
 

time: 124 us -> 124 us (level)
  no operation moved by 1% of the time
where the time goes in v9:
time: 124 us
  blocking collectives  108 us (87%)
  Pallas kernels  10.1 us (8%)
  starting transfers between devices  4.43 us (4%)
    all_to_all x1, blocking collectives, on_device(): lax.all_to_all(pack(signal, upstream, long_filter, parts), 'seq', 0, 0, t...  64 us
    all_to_all x1, blocking collectives, on_device(): lax.all_to_all(stamp(message, short, squares), 'seq', 0, 0, tiled=True)  43.7 us
    all_to_all x1, starting transfers between devices, on_device(): squares = lax.all_to_all(squares, 'ch', 0, 0, tiled=True)  4.43 us
    pallas_call x1, Pallas kernels, signal_side(): pl.pallas_call(signal_side_kernel, out_shape=(jax.ShapeDtypeStruct((block...  4.42 us
    pallas_call x1, Pallas kernels, filter_side(): pl.pallas_call(filter_side_kernel, out_shape=(jax.ShapeDtypeStruct((count...  2.89 us
  transfers between devices with their start and end apart: 1, of which 1 were waited for; matrix products, arithmetic and copies ran while one was open for 0% of the time, Pallas kernels for 4%

profile of v9, /device:TPU:32, one launch (start us, length us, event | category | flops | bytes accessed | tf_op | source)
XLA Modules:
  0.0 123.8 jit_solution(3053553900515249017)
XLA Ops:
  0.6 1.4 %shard_map.103 = bf16[128,24,128]{2,1,0:T(8,128)(2,1)S(1)} custom-call(bf16[128,1024]{1,0:T(8,128)(2,1)} %first_ref.1, bf16[128,1024]{1,0:T(8,128)(2,1)} %second_ref.1, bf16[128,1024]{1,0:T(8,128)(2,1)} %third_ref.1), custom_call_target="tpu_custom_call" | custom-call | flops 1000000 | bytes 1572864 | tf_op jit(solution)/shard_map/pallas_call | solution.py:305
  2.0 0.0 copy-start
  2.0 0.0 copy-start.2
  2.0 0.0 copy-start.3
  2.0 0.0 copy-start.4
  2.0 64.0 %all_to_all.15.got_ref = bf16[128,24,128]{2,1,0:T(8,128)(2,1)S(1)} all-to-all(bf16[128,24,128]{2,1,0:T(8,128)(2,1)S(1)} %shard_map.103), channel_id=1, replica_groups=mesh['seq'=128,'ch'=4] {'seq'}, dimensions={0} | all-to-all | bytes 1572864 | tf_op jit(solution)/shard_map/all_to_all | solution.py:357
  66.0 0.0 copy-done
  66.0 0.0 copy-done.2
  66.0 0.0 copy-done.3
  66.0 0.0 copy-done.4
  66.0 2.9 %shard_map.104 = (f32[1024,256]{1,0:T(8,128)S(1)}, bf16[8,128,128]{2,1,0:T(8,128)(2,1)S(1)}, f32[4,1,128]{2,1,0:T(1,128)}) custom-call(bf16[128,24,128]{2,1,0:T(8,128)(2,1)S(1)} %all_to_all.15.got_ref, bf16[64,128]{1,0:T(8,128)(2,1)S(1)} %bitcast.2, bf16[256,256]{1,0:T(8,128)(2,1)S(1)} %copy-done.4, f32[2,128,128]{2,1,0:T(8,128)S(1)} %copy-done.3, ...), custom_call_target="tpu_custom_call" | custom-call | flops 3000000000 | bytes 6000000 | tf_op jit(solution)/shard_map/pallas_call | solution.py:218
  68.9 0.0 copy-start.1
  68.9 4.4 %all-to-all-start.1 = ((f32[4,1,128]{2,1,0:T(1,128)}), f32[4,1,128]{2,1,0:T(1,128)S(1)}, u32[]{:S(2)}, u32[]{:S(2)}) async-start(f32[4,1,128]{2,1,0:T(1,128)} %get-tuple-element.15), calls=%async_computation.1 | async-start | bytes 4096 | tf_op jit(solution)/shard_map/all_to_all | solution.py:360
  73.3 0.0 copy-done.1
  73.3 4.4 %shard_map.105 = (bf16[128,9,2,128]{3,2,1,0:T(2,128)(2,1)S(1)}, f32[8,128]{1,0:T(8,128)S(1)}) custom-call(bf16[128,24,128]{2,1,0:T(8,128)(2,1)S(1)} %all_to_all.15.got_ref, f32[1024,256]{1,0:T(8,128)S(1)} %get-tuple-element.11.spectrum_ref, bf16[8,128,128]{2,1,0:T(8,128)(2,1)S(1)} %get-tuple-element.12.raw_ref, bf16[64,128]{1,0:T(8,128)(2,1)S(1)} %bitcast.3, ...), custom_call_target="tpu_custom_call" | custom-call | flops 3000000000 | bytes 6000000 | tf_op jit(solution)/shard_map/pallas_call | solution.py:239
  77.8 0.8 all-to-all-done.1.squares_ref
  78.5 0.1 shard_map.106
  78.6 43.7 %all_to_all.16.refs_0_ = bf16[128,9,2,128]{3,2,1,0:T(2,128)(2,1)S(1)} all-to-all(bf16[128,9,2,128]{3,2,1,0:T(2,128)(2,1)S(1)} %shard_map.106), channel_id=1, replica_groups=mesh['seq'=128,'ch'=4] {'seq'}, dimensions={0} | all-to-all | bytes 1179648 | tf_op jit(solution)/shard_map/all_to_all | solution.py:362
  122.4 1.4 %shard_map.107 = (bf16[128,1024]{1,0:T(8,128)(2,1)}, bf16[128,1024]{1,0:T(8,128)(2,1)}, f32[64,128]{1,0:T(8,128)}) custom-call(bf16[128,9,2,128]{3,2,1,0:T(2,128)(2,1)S(1)} %all_to_all.16.refs_0_), custom_call_target="tpu_custom_call" | custom-call | tf_op jit(solution)/shard_map/pallas_call | solution.py:336
Async XLA Ops:
  2.0 64.0 %copy-start = (bf16[128,64]{0,1:T(8,128)(2,1)S(1)}, bf16[128,64]{0,1:T(8,128)(2,1)}, u32[]{:S(2)}) copy-start(bf16[128,64]{0,1:T(8,128)(2,1)} %param.11) | copy-start | bytes 49156
  2.0 64.0 %copy-start.2 = (bf16[2,256,256]{2,1,0:T(8,128)(2,1)S(1)}, bf16[2,256,256]{2,1,0:T(8,128)(2,1)}, u32[]{:S(2)}) copy-start(bf16[2,256,256]{2,1,0:T(8,128)(2,1)} %constant.8.clone.inner_ref) | copy-start | bytes 786436
  2.0 64.0 %copy-start.3 = (f32[2,128,128]{2,1,0:T(8,128)S(1)}, f32[2,128,128]{2,1,0:T(8,128)}, u32[]{:S(2)}) copy-start(f32[2,128,128]{2,1,0:T(8,128)} %constant.7.clone.twist_ref) | copy-start | bytes 393220
  2.0 64.0 %copy-start.4 = (bf16[256,256]{1,0:T(8,128)(2,1)S(1)}, bf16[256,256]{1,0:T(8,128)(2,1)}, u32[]{:S(2)}) copy-start(bf16[256,256]{1,0:T(8,128)(2,1)} %constant.6.clone.enter_ref) | copy-start | bytes 393220
  68.9 4.4 %copy-start.1 = (f32[1024]{0:T(1024)S(1)}, f32[1024]{0:T(1024)}, u32[]{:S(2)}) copy-start(f32[1024]{0:T(1024)} %skip_ref.1) | copy-start | bytes 12292
  68.9 9.6 %all-to-all-start.1 = ((f32[4,1,128]{2,1,0:T(1,128)}), f32[4,1,128]{2,1,0:T(1,128)S(1)}, u32[]{:S(2)}, u32[]{:S(2)}) async-start(f32[4,1,128]{2,1,0:T(1,128)} %get-tuple-element.15), calls=%async_computation.1 | async-start | bytes 4096 | tf_op jit(solution)/shard_map/all_to_all | solution.py:360
